TPU v7x, 128 devices: a whole 4x4x4 slice. The times are simulated.
128 devices in a mesh: dp: 4 (over z), fsdp: 32 (over x, y, core).
Axes of the slice: x: 4, y: 4, z: 4, core: 2. Of those that a mesh axis runs over, the one named last changes fastest.
Arguments:
- weight_up: bfloat16 [8192, 16384], P('dp', 'fsdp'), may hold values from -6 to 6
- weight_down: bfloat16 [16384, 8192], P('dp', 'fsdp'), may hold values from -6 to 6
- grad_up: bfloat16 [4, 8192, 16384], P('dp', None, 'fsdp'), may hold values from -6 to 6
- grad_down: bfloat16 [4, 16384, 8192], P('dp', None, 'fsdp'), may hold values from -8 to 8
- basis_up: bfloat16 [8192, 256], P('fsdp'), may hold values from -0.0625 to 0.0625
- basis_down: bfloat16 [8192, 256], P('fsdp'), may hold values from -0.0625 to 0.0625
- moment_up: float32 [256, 16384], P('dp', 'fsdp'), may hold values from -4 to 4
- second_up: float32 [256, 16384], P('dp', 'fsdp'), may hold values from 0.2 to 2
- moment_down: float32 [16384, 256], P(('dp', 'fsdp')), may hold values from -4 to 4
- second_down: float32 [16384, 256], P(('dp', 'fsdp')), may hold values from 0.2 to 2
Outputs:
- new_weight_up: bfloat16 [8192, 16384], P('dp', 'fsdp')
- new_weight_down: bfloat16 [16384, 8192], P('dp', 'fsdp')
- new_moment_up: float32 [256, 16384], P('dp', 'fsdp')
- new_second_up: float32 [256, 16384], P('dp', 'fsdp')
- new_moment_down: float32 [16384, 256], P(('dp', 'fsdp'))
- new_second_down: float32 [16384, 256], P(('dp', 'fsdp'))
All inputs are finite; a program needn't handle non-finite values.
Results may differ from a plain program's by a relative error of at most 0.0055.
Values may be sent and summed in bfloat16 or wider, within the bound.
No kernel may reach another device: no remote copies, remote signals or barrier semaphores. Data moves between devices by JAX's collectives and lax.ppermute only.
A program may use at most 128 MiB of HBM per device.

v0:
```python
import jax
import jax.numpy as jnp
from jax import lax
from jax.sharding import PartitionSpec as P

ADAM_STEP = 10


first_decay = 0.9
second_decay = 0.99
adam_eps = 1e-08
norm_eps = 1e-06
learn_rate = 0.5


def adam_update(mean_grad, first, second):
    new_first = first_decay * first + (1.0 - first_decay) * mean_grad
    new_second = second_decay * second + (1.0 - second_decay) * mean_grad * mean_grad
    corr_first = 1.0 - first_decay**ADAM_STEP
    corr_second = 1.0 - second_decay**ADAM_STEP
    update = (new_first / corr_first / (jnp.sqrt(new_second / corr_second) + adam_eps)).astype(
        jnp.bfloat16
    )
    return (new_first, new_second, update)


def per_device(
    weight_up,
    weight_down,
    grad_up,
    grad_down,
    basis_up,
    basis_down,
    moment_up,
    second_up,
    moment_down,
    second_down,
):
    replicas = lax.axis_size("dp")
    local_up = grad_up[0]
    local_down = grad_down[0]
    weight_upf = weight_up.astype(jnp.float32)
    weight_downf = weight_down.astype(jnp.float32)
    wsq_up = jnp.sum(weight_upf * weight_upf)
    wsq_down = jnp.sum(weight_downf * weight_downf)
    full_basis = lax.all_gather(basis_up, "fsdp", axis=0, tiled=True)
    columns = full_basis
    proj_up = lax.psum_scatter(
        lax.dot_general(
            columns, local_up, (((0,), (0,)), ((), ())), preferred_element_type=jnp.float32
        ).astype(jnp.bfloat16),
        "dp",
        scatter_dimension=0,
        tiled=True,
    ).astype(jnp.float32) * (1.0 / replicas)
    new_moment_up, new_second_up, low_up = adam_update(proj_up, moment_up, second_up)
    proj_down = lax.psum_scatter(
        jnp.dot(local_down, basis_down, preferred_element_type=jnp.float32),
        ("dp", "fsdp"),
        scatter_dimension=0,
        tiled=True,
    )
    proj_down = proj_down * (1.0 / replicas)
    new_moment_down, new_second_down, low_down = adam_update(proj_down, moment_down, second_down)
    block_rows = full_basis.shape[0] // replicas
    basis_block = lax.dynamic_slice_in_dim(
        full_basis, lax.axis_index("dp") * block_rows, block_rows, 0
    )
    delta_down = lax.dot_general(
        lax.all_gather(low_down, "fsdp", axis=0, tiled=True),
        basis_down,
        (((1,), (1,)), ((), ())),
        preferred_element_type=jnp.float32,
    )
    columns = basis_block
    delta_up = jnp.dot(
        columns,
        lax.all_gather(low_up, "dp", axis=0, tiled=True),
        preferred_element_type=jnp.float32,
    )
    dsq_up = jnp.sum(delta_up * delta_up)
    dsq_down = jnp.sum(delta_down * delta_down)
    local_sums = (wsq_up, wsq_down, dsq_up, dsq_down)
    total_wup, total_wdown, total_dup, total_ddown = lax.psum(
        (local_sums[0], local_sums[1], local_sums[2], local_sums[3]), ("dp", "fsdp")
    )
    ratio_up = jnp.sqrt(total_wup) / (jnp.sqrt(total_dup) + norm_eps)
    ratio_down = jnp.sqrt(total_wdown) / (jnp.sqrt(total_ddown) + norm_eps)
    new_weight_up = (weight_upf - learn_rate * ratio_up * delta_up).astype(jnp.bfloat16)
    new_weight_down = (weight_downf - learn_rate * ratio_down * delta_down).astype(jnp.bfloat16)
    return (
        new_weight_up,
        new_weight_down,
        new_moment_up,
        new_second_up,
        new_moment_down,
        new_second_down,
    )


def solution(mesh):
    in_specs = (
        P("dp", "fsdp"),
        P("dp", "fsdp"),
        P("dp", None, "fsdp"),
        P("dp", None, "fsdp"),
        P("fsdp", None),
        P("fsdp", None),
        P("dp", "fsdp"),
        P("dp", "fsdp"),
        P(("dp", "fsdp"), None),
        P(("dp", "fsdp"), None),
    )
    out_specs = (
        P("dp", "fsdp"),
        P("dp", "fsdp"),
        P("dp", "fsdp"),
        P("dp", "fsdp"),
        P(("dp", "fsdp"), None),
        P(("dp", "fsdp"), None),
    )
    return jax.shard_map(
        per_device, mesh=mesh, in_specs=in_specs, out_specs=out_specs, check_vma=False
    )
```

profile of v0, /device:TPU:1, one launch (start us, length us, event | category | flops | bytes accessed | tf_op | source)
XLA Modules:
  0.0 818.7 jit_solution(4987437287833682220)
XLA Ops:
  8.0 0.0 copy-start
  8.0 0.0 all-gather.3.cloned.1.call-start
  8.1 0.7 all-gather.3.cloned.1.call-update
  8.7 0.0 reduce-scatter.5.cloned.1.call-start
  8.8 0.1 copy-done
  8.9 11.5 %fusion = f32[16384,256]{1,0:T(8,128)} fusion(bf16[256,256]{1,0:T(8,128)(2,1)S(1)} %copy-done, bf16[1,16384,256]{2,1,0:T(8,128)(2,1)} %param.13), kind=kOutput, calls=%fused_computation | convolution fusion | flops 2147483648 | bytes 25296896 | tf_op jit(solution)/shard_map/dot_general | solution.py:58
  20.4 0.0 reduce-scatter.5.cloned.1.call-update
  20.4 0.0 copy-start.6
  20.4 0.0 copy-start.7
  20.4 0.0 copy-start.2
  20.4 0.0 reduce-scatter.3.cloned.1.call-start
  20.5 41.5 %all-gather.3.cloned.1.call-done = bf16[8192,256]{1,0:T(8,128)(2,1)} async-done(((bf16[256,256]{1,0:T(8,128)(2,1)}), bf16[8192,256]{1,0:T(8,128)(2,1)}) %all-gather.3.cloned.1.call-update) | async-done | bytes 4194320 | tf_op jit(solution)/shard_map/all_gather | solution.py:46
  62.0 7.8 fusion.8
  69.8 0.0 reduce-scatter.3.cloned.1.call-update
  69.8 0.0 all-gather.5.cloned.1.call-start
  69.8 615.9 %reduce-scatter.5.cloned.1.call-done = f32[128,256]{1,0:T(8,128)} async-done(((f32[16384,256]{1,0:T(8,128)}), f32[128,256]{1,0:T(8,128)}) %reduce-scatter.5.cloned.1.call-update) | async-done | bytes 131088 | tf_op jit(solution)/shard_map/reduce_scatter | solution.py:57
  685.7 0.0 copy-done.7
  685.7 1.7 divide_convert_fusion
  687.4 0.0 all-gather.5.cloned.1.call-update
  687.4 0.0 copy-done.2
  687.4 1.7 fusion.4
  689.1 3.2 fusion.6
  692.4 15.8 %reduce-scatter.3.cloned.1.call-done = bf16[64,512]{1,0:T(8,128)(2,1)} async-done(((bf16[256,512]{1,0:T(8,128)(2,1)}), bf16[64,512]{1,0:T(8,128)(2,1)}) %reduce-scatter.3.cloned.1.call-update) | async-done | bytes 65552 | tf_op jit(solution)/shard_map/reduce_scatter | solution.py:48
  708.2 1.6 divide_convert_fusion.1
  709.8 9.9 %all_gather.10 = bf16[256,512]{1,0:T(8,128)(2,1)S(1)} all-gather(bf16[64,512]{1,0:T(8,128)(2,1)S(1)} %get-tuple-element.13), channel_id=1, replica_groups=mesh['dp'=4,'fsdp'=32] {'dp'}, dimensions={0}, use_global_device_ids=true | all-gather | bytes 327680 | tf_op jit(solution)/shard_map/all_gather | solution.py:78
  719.7 4.9 multiply_reduce_fusion.1
  724.6 7.7 all-gather.5.cloned.1.call-done
  732.3 5.4 multiply_reduce_fusion
  737.6 64.5 %all-reduce = (f32[]{:T(128)}, f32[]{:T(128)}, f32[]{:T(128)}, f32[]{:T(128)}) all-reduce(f32[]{:T(128)} %fusion.4, f32[]{:T(128)} %get-tuple-element.16, f32[]{:T(128)} %fusion.6, f32[]{:T(128)} %get-tuple-element.18), channel_id=1, replica_groups=mesh['dp'=4,'fsdp'=32] {'dp','fsdp'}, use_global_device_ids=true, to_apply=%region_1.0 | all-reduce | flops 4 | bytes 32 | tf_op jit(solution)/shard_map/psum | solution.py:84
  804.9 0.0 copy-start.3
  804.9 4.4 fusion.5
  809.3 1.9 fusion.7
  (8 shorter events, 0.0 us)
Async XLA Ops:
  8.0 0.9 copy-start
  8.0 54.0 %all-gather.3.cloned.1.call-start = ((), (), s32[]{:S(2)}) async-start(), calls=%async_computation.2 | async-start | bytes 4325376 | tf_op jit(solution)/shard_map/all_gather | solution.py:46
  8.7 677.0 %reduce-scatter.5.cloned.1.call-start = ((), (), s32[]{:S(2)}) async-start(), calls=%async_computation.4 | async-start | bytes 16908288 | tf_op jit(solution)/shard_map/reduce_scatter | solution.py:57
  20.4 665.3 %copy-start.6 = (f32[128,256]{1,0:T(8,128)S(1)}, f32[128,256]{1,0:T(8,128)}, u32[]{:S(2)}) copy-start(f32[128,256]{1,0:T(8,128)} %param.18) | copy-start | bytes 393220
  20.4 665.3 %copy-start.7 = (f32[128,256]{1,0:T(8,128)S(1)}, f32[128,256]{1,0:T(8,128)}, u32[]{:S(2)}) copy-start(f32[128,256]{1,0:T(8,128)} %param.19) | copy-start | bytes 393220
  20.4 667.0 %copy-start.2 = (bf16[2048,512]{1,0:T(8,128)(2,1)S(1)}, bf16[2048,512]{1,0:T(8,128)(2,1)}, u32[]{:S(2)}) copy-start(bf16[2048,512]{1,0:T(8,128)(2,1)} %param.10) | copy-start | bytes 6291460
  20.4 687.8 %reduce-scatter.3.cloned.1.call-start = ((), (), s32[]{:S(2)}) async-start(), calls=%async_computation.3 | async-start | bytes 327680 | tf_op jit(solution)/shard_map/reduce_scatter | solution.py:48
  69.8 638.4 %copy-start.4 = (f32[64,512]{1,0:T(8,128)S(1)}, f32[64,512]{1,0:T(8,128)}, u32[]{:S(2)}) copy-start(f32[64,512]{1,0:T(8,128)} %param.16) | copy-start | bytes 393220
  69.8 638.4 %copy-start.5 = (f32[64,512]{1,0:T(8,128)S(1)}, f32[64,512]{1,0:T(8,128)}, u32[]{:S(2)}) copy-start(f32[64,512]{1,0:T(8,128)} %param.17) | copy-start | bytes 393220
  69.8 662.5 %all-gather.5.cloned.1.call-start = ((), (), s32[]{:S(2)}) async-start(), calls=%async_computation.5 | async-start | bytes 2162688 | tf_op jit(solution)/shard_map/all_gather | solution.py:70
  804.9 4.4 copy-start.1
  804.9 4.4 copy-start.3
Sparse Core Ops, SparseCore 0:
  11.1 50.8 all-gather.2
  687.5 44.6 all-gather.4
Sparse Core Ops, SparseCore 1:
  20.5 665.2 reduce-scatter.4
  688.5 19.6 reduce-scatter.2
where the time goes:
time: 819 us
  waiting for transfers between devices  682 us (83%)
  blocking collectives  74.4 us (9%)
  matrix products  29.5 us (4%)
  between operations  18.3 us (2%)
  other arithmetic  14.5 us (2%)
    reduce_scatter x1, waiting for transfers between devices, per_device(): lax.psum_scatter(jnp.dot(local_down, basis_down, preferred_element_type=j...  616 us
    psum x1, blocking collectives, per_device(): lax.psum((local_sums[0], local_sums[1], local_sums[2], local_sums[3]), ('...  64.5 us
    all_gather x1, waiting for transfers between devices, per_device(): full_basis = lax.all_gather(basis_up, 'fsdp', axis=0, tiled=True)  41.5 us
  transfers between devices with their start and end apart: 4, of which 4 were waited for; matrix products, arithmetic and copies ran while one was open for 4% of the time, Pallas kernels for 0%

commit v1 on v0

v1 whole, which is shorter than its diff:
```python
import functools

import jax
import jax.numpy as jnp
from jax import lax
from jax.experimental import pallas as pl
from jax.experimental.pallas import tpu as pltpu
from jax.sharding import Mesh, PartitionSpec as P

ADAM_STEP = 10

first_decay = 0.9
second_decay = 0.99
adam_eps = 1e-08
norm_eps = 1e-06
learn_rate = 0.5

f32 = jnp.float32
bf16 = jnp.bfloat16

AXES = ("z", "x", "y", "c")
SIZES = (4, 4, 4, 2)


def adam_update(mean_grad, first, second):
    new_first = first_decay * first + (1.0 - first_decay) * mean_grad
    new_second = second_decay * second + (1.0 - second_decay) * mean_grad * mean_grad
    corr_first = 1.0 - first_decay**ADAM_STEP
    corr_second = 1.0 - second_decay**ADAM_STEP
    update = (new_first / corr_first / (jnp.sqrt(new_second / corr_second) + adam_eps)).astype(
        bf16
    )
    return (new_first, new_second, update)


def shift_pairs(axis0, axis1, k):
    pairs = []
    for source in range(128):
        coords = [source // 32, source // 8 % 4, source // 2 % 4, source % 2]
        dim = AXES.index(axis1 if coords[3] else axis0)
        coords[dim] = (coords[dim] + k) % 4
        target = ((coords[0] * 4 + coords[1]) * 4 + coords[2]) * 2 + coords[3]
        pairs.append((source, target))
    return pairs


def shift(value, axis0, axis1, k):
    return lax.ppermute(value, AXES, shift_pairs(axis0, axis1, k))


def swap_cores(value):
    return lax.ppermute(value, "c", [(0, 1), (1, 0)])


def pick(stacked, index):
    return lax.dynamic_index_in_dim(stacked, index, 0, keepdims=False)


def place_of(place, own):
    return place[2] if own else 1 - place[2]


def project_kernel(has_other, place_ref, *refs):
    grad_refs, basis_ref, out_ref = refs[:4], refs[4], refs[-1]
    for part, grad_ref in enumerate(grad_refs):
        rows = grad_ref[...].reshape(512, 256)
        out = jnp.dot(rows, basis_ref[...], preferred_element_type=f32)
        if has_other:
            out = out + refs[5][0, part].reshape(512, 256).astype(f32)
        out_ref[0, part] = out.astype(bf16).reshape(4, 128, 256)


def project_rows(place, grad, basis, own, shifts, other=None, other_at=0):
    def grad_map(part):
        def index(step, place):
            core = place_of(place, own)
            ahead = shifts[-1]
            for i, shift_by in enumerate(shifts[:-1]):
                ahead = jnp.where(step == i, shift_by, ahead)
            block = (jnp.where(core == 0, place[0], place[1]) + ahead) % 4
            return (
                jnp.where(core == 0, block, part),
                jnp.where(core == 0, part, block),
                0,
                core,
                0,
                0,
            )

        return index

    tile = (1, 4, 4, 128, 256)
    in_specs = [pl.BlockSpec((1, 1, 4, 1, 128, 256), grad_map(part)) for part in range(4)]
    in_specs.append(pl.BlockSpec((256, 256), lambda step, place: (0, 0)))
    operands = [place, grad, grad, grad, grad, basis]
    if other is not None:
        in_specs.append(pl.BlockSpec(tile, lambda step, place: (other_at, 0, 0, 0, 0)))
        operands.append(other)
    count = len(shifts)
    return pl.pallas_call(
        functools.partial(project_kernel, other is not None),
        out_shape=jax.ShapeDtypeStruct((count, 4, 4, 128, 256), bf16),
        grid_spec=pltpu.PrefetchScalarGridSpec(
            num_scalar_prefetch=1,
            grid=(count,),
            in_specs=in_specs,
            out_specs=pl.BlockSpec(tile, lambda step, place: (step, 0, 0, 0, 0)),
        ),
        compiler_params=pltpu.CompilerParams(vmem_limit_bytes=24 << 20),
        cost_estimate=pl.CostEstimate(
            flops=count, bytes_accessed=count, transcendentals=0
        ),
    )(*operands)


def project_up_kernel(place_ref, basis_ref, *refs):
    grad_refs, before_ref, out_ref, sum_ref = refs[:8], refs[8:-2], refs[-2], refs[-1]
    step = pl.program_id(0)

    @pl.when(step == 0)
    def _():
        sum_ref[...] = before_ref[0][...] if before_ref else jnp.zeros_like(sum_ref)

    parts = [
        lax.dot_general(
            basis_ref[part // 4, part % 4],
            grad_ref[...],
            (((0,), (0,)), ((), ())),
            preferred_element_type=f32,
        )
        for part, grad_ref in enumerate(grad_refs)
    ]
    sum_ref[...] += functools.reduce(lambda a, b: a + b, parts)

    @pl.when(step == 1)
    def _():
        out_ref[...] = sum_ref[...].astype(out_ref.dtype)


def project_up(place, basis, grad, own, before=None):
    def grad_map(part):
        def index(step, place):
            x = (place[1] + 4 - part % 4) % 4
            y = (place[3] + 4 - part // 4 - 2 * step) % 4
            return ((x * 4 + y) * 2 + place_of(place, own), 0)

        return index

    whole = pl.BlockSpec((256, 512), lambda step, place: (0, 0))
    in_specs = [pl.BlockSpec((2, 4, 256, 256), lambda step, place: (step, 0, 0, 0))]
    in_specs += [pl.BlockSpec((256, 512), grad_map(part)) for part in range(8)]
    operands = [place, basis] + [grad] * 8
    if before is not None:
        in_specs.append(whole)
        operands.append(before)
    return pl.pallas_call(
        project_up_kernel,
        out_shape=jax.ShapeDtypeStruct((256, 512), f32 if before is None else bf16),
        grid_spec=pltpu.PrefetchScalarGridSpec(
            num_scalar_prefetch=1,
            grid=(2,),
            in_specs=in_specs,
            out_specs=whole,
            scratch_shapes=[pltpu.VMEM((256, 512), f32)],
        ),
        compiler_params=pltpu.CompilerParams(vmem_limit_bytes=60 << 20),
        cost_estimate=pl.CostEstimate(
            flops=1, bytes_accessed=1, transcendentals=0
        ),
    )(*operands)


def sum_kernel(place_ref, own_ref, *refs):
    got_refs, next_ref, out_refs = refs[:3], refs[3], refs[4:]
    start = jnp.where(place_ref[2] == 0, place_ref[1], place_ref[0])
    for ahead, out_ref in zip((0, 2, 1, 3), (next_ref, *out_refs), strict=True):
        at = (start + ahead) % 4
        value = own_ref[at].astype(f32)
        for got_ref in got_refs:
            value = value + got_ref[at].astype(f32)
        out_ref[...] = value.astype(out_ref.dtype)


def sum_blocks(place, own, got):
    vmem = pl.BlockSpec(memory_space=pltpu.VMEM)
    block = jax.ShapeDtypeStruct((4, 128, 256), bf16)
    return pl.pallas_call(
        sum_kernel,
        out_shape=[jax.ShapeDtypeStruct((4, 128, 256), f32), block, block, block],
        in_specs=[pl.BlockSpec(memory_space=pltpu.SMEM)] + [vmem] * 4,
        out_specs=[vmem] * 4,
        compiler_params=pltpu.CompilerParams(vmem_limit_bytes=24 << 20),
        cost_estimate=pl.CostEstimate(flops=4 << 20, bytes_accessed=5 << 20, transcendentals=0),
    )(place, own, *got)


def norms_kernel(weights_ref, *refs):
    low_refs, (basis_down_ref, other_down_ref) = refs[:4], refs[4:6]
    own_ref, other_ref, low_up_ref, out_ref = refs[6:]

    def square_sum(delta):
        return jnp.sum(jnp.sum(delta * delta, axis=0, keepdims=True), axis=1, keepdims=True)

    up = jnp.zeros((1, 1), f32)
    for ref in (own_ref, other_ref):
        for block in range(4):
            up += square_sum(jnp.dot(ref[block], low_up_ref[...], preferred_element_type=f32))
    down = jnp.zeros((1, 1), f32)
    for low_ref in low_refs:
        for ref in (basis_down_ref, other_down_ref):
            down += square_sum(
                lax.dot_general(
                    low_ref[...].reshape(512, 256),
                    ref[...],
                    (((1,), (1,)), ((), ())),
                    preferred_element_type=f32,
                )
            )
    lane = lax.broadcasted_iota(jnp.int32, (1, 128), 1)
    row = jnp.where(lane == 0, weights_ref[0], weights_ref[1])
    row = jnp.where(lane == 2, up, jnp.where(lane == 3, down, row))
    out_ref[...] = jnp.broadcast_to(row[None], out_ref.shape)


def norms(weight_sums, lows, basis_down, other_down, own, other, low_up):
    vmem = pl.BlockSpec(memory_space=pltpu.VMEM)
    operands = [weight_sums, *lows, basis_down, other_down, own, other, low_up]
    return pl.pallas_call(
        norms_kernel,
        out_shape=jax.ShapeDtypeStruct((128, 1, 128), f32),
        in_specs=[pl.BlockSpec(memory_space=pltpu.SMEM)] + [vmem] * (len(operands) - 1),
        out_specs=vmem,
        compiler_params=pltpu.CompilerParams(vmem_limit_bytes=16 << 20),
        cost_estimate=pl.CostEstimate(
            flops=1 << 34, bytes_accessed=3 << 20, transcendentals=0
        ),
    )(*operands)


def update_kernel(place_ref, sums_ref, *refs):
    low_refs, (basis_down_ref, weight_down_ref) = refs[:8], refs[8:10]
    own_ref, other_ref, low_up_ref, weight_up_ref, up_ref, down_ref = refs[10:]
    sums = jnp.sum(sums_ref[...], axis=0)
    scale_up = learn_rate * (jnp.sqrt(sums[:, 0:1]) / (jnp.sqrt(sums[:, 2:3]) + norm_eps))
    scale_down = learn_rate * (jnp.sqrt(sums[:, 1:2]) / (jnp.sqrt(sums[:, 3:4]) + norm_eps))
    core0 = place_ref[2]
    for back in range(4):
        y = (place_ref[3] + 4 - back) % 4
        for basis_ref, core in ((own_ref, core0), (other_ref, 1 - core0)):
            delta = jnp.dot(basis_ref[back], low_up_ref[...], preferred_element_type=f32)
            old = weight_up_ref[y, core].astype(f32)
            up_ref[y, core] = (old - scale_up * delta).astype(bf16)
    for i, low_ref in enumerate(low_refs):
        outer = i % 4
        core = core0 if i < 4 else 1 - core0
        delta = lax.dot_general(
            low_ref[...].reshape(512, 256),
            basis_down_ref[...],
            (((1,), (1,)), ((), ())),
            preferred_element_type=f32,
        )
        for inner in range(4):
            x = (place_ref[1] + 4 - jnp.where(core == 0, outer, inner)) % 4
            y = (place_ref[3] + 4 - jnp.where(core == 0, inner, outer)) % 4
            old = weight_down_ref[x, y, core].astype(f32)
            down_ref[x, y, core] = (
                old - scale_down * delta[inner * 128 : (inner + 1) * 128]
            ).astype(bf16)


def update(place, sums, lows, basis_down, weight_down, own, other, low_up, weight_up):
    vmem = pl.BlockSpec(memory_space=pltpu.VMEM)
    operands = [place, sums, *lows, basis_down, weight_down, own, other, low_up, weight_up]
    return pl.pallas_call(
        update_kernel,
        out_shape=[
            jax.ShapeDtypeStruct(weight_up.shape, bf16),
            jax.ShapeDtypeStruct(weight_down.shape, bf16),
        ],
        in_specs=[pl.BlockSpec(memory_space=pltpu.SMEM)] + [vmem] * (len(operands) - 1),
        out_specs=[vmem, vmem],
        compiler_params=pltpu.CompilerParams(vmem_limit_bytes=16 << 20),
        cost_estimate=pl.CostEstimate(
            flops=4 * 2048 * 256 * 512, bytes_accessed=11 << 20, transcendentals=0
        ),
    )(*operands)


def after(value, *others):
    return lax.optimization_barrier((value, *others))[0]


def total(stages, first):
    return functools.reduce(lambda a, b: a + b.astype(f32), stages, first.astype(f32))


def per_device(
    weight_up,
    weight_down,
    grad_up,
    grad_down,
    basis_up,
    basis_down,
    moment_up,
    second_up,
    moment_down,
    second_down,
):
    z, x, y, c = (lax.axis_index(a) for a in AXES)
    replicas = 4
    local_up = grad_up[0]
    local_down = grad_down[0].reshape(4, 4, 4, 2, 128, 256)

    place = jnp.stack([z, x, c, y]).astype(jnp.int32)

    near = jnp.stack([basis_up] + [shift(basis_up, "x", "x", k) for k in (1, 2, 3)])
    weight_upf = weight_up.astype(f32)
    weight_downf = weight_down.astype(f32)
    wsq_up = jnp.sum(weight_upf * weight_upf)
    wsq_down = jnp.sum(weight_downf * weight_downf)

    other_basis_down = swap_cores(basis_down)
    place = after(place, other_basis_down)
    half = functools.partial(project_rows, place, local_down, basis_down, False)
    whole = functools.partial(project_rows, place, local_down, basis_down, True)
    half_2 = half((2,))
    got_2 = swap_cores(half_2)
    ready = {2: whole((2,), got_2)[0]}
    half_130 = project_rows(
        after(place, half_2, near), local_down, basis_down, False, (1, 3, 0)
    )
    got_130 = swap_cores(half_130)
    ready[1] = whole((1,), got_130, 0)[0]
    ready[3] = whole((3,), after(got_130, ready[1]), 1)[0]
    ready[0] = whole((0,), after(got_130, ready[3]), 2)[0]
    one = [shift(ready[k], "z", "x", k) for k in (2, 1, 3)]

    two_own, *two = sum_blocks(after(place, wsq_up, wsq_down), ready[0], one)
    two = [two_own] + [shift(t, "x", "z", k) for t, k in zip(two, (2, 1, 3))]

    back, ahead = shift(near, "y", "y", 1), shift(near, "y", "y", 3)
    back_half, ahead_half = after(back[:2], two[0]), after(ahead[2:], two[0])
    far = jnp.concatenate([shift(back_half, "y", "y", 1), shift(ahead_half, "y", "y", 3)])
    own_basis = jnp.stack([near, back, far, ahead])
    own_basis = after(own_basis, *two[1:])
    other_basis = swap_cores(own_basis)

    partial_up = project_up(place, own_basis, local_up, True)
    two[0] = after(two[0], partial_up)
    partial_up = project_up(place, other_basis, local_up, False, partial_up)
    partial_up = partial_up.reshape(4, 64, 512)

    def part_three(k):
        index = (y + k) % 4
        return total([pick(t, index) for t in two[1:]], pick(two[0], index))

    three = [part_three(0)] + [
        shift(part_three(k).astype(bf16), "y", "y", k) for k in (2, 1, 3)
    ]
    three[0] = after(three[0], partial_up)
    proj_down = total(three[1:], three[0]) * (1.0 / replicas)
    new_moment_down, new_second_down, low_down = adam_update(proj_down, moment_down, second_down)

    up = [pick(partial_up, z)] + [
        shift(pick(partial_up, (z + k) % 4), "z", "z", k) for k in (2, 1, 3)
    ]
    proj_up = total(up[1:], up[0]) * (1.0 / replicas)
    new_moment_up, new_second_up, low_up = adam_update(proj_up, moment_up, second_up)
    gathered = jnp.stack([low_up] + [shift(low_up, "z", "z", k) for k in (1, 2, 3)])
    gathered = jnp.stack([pick(gathered, (z + 4 - block) % 4) for block in range(4)])
    all_low_up = gathered.reshape(256, 512)

    blocks = [
        lax.dynamic_index_in_dim(basis, (x + 4 - z) % 4, 1, keepdims=False)
        for basis in (own_basis, other_basis)
    ]

    inner = jnp.stack([low_down] + [shift(low_down, "y", "x", k) for k in (1, 2, 3)])
    outer = [inner] + [shift(inner, "x", "y", k) for k in (1, 2, 3)]
    sibling = [swap_cores(low) for low in outer]

    sums = norms(
        jnp.stack([wsq_up, wsq_down]),
        outer,
        basis_down,
        other_basis_down,
        *blocks,
        all_low_up,
    )
    sums = lax.all_to_all(sums, AXES, 0, 0, tiled=True)
    new_weight_up, new_weight_down = update(
        place,
        sums,
        outer + sibling,
        basis_down,
        weight_down.reshape(4, 4, 2, 128, 256),
        *blocks,
        all_low_up,
        weight_up.reshape(4, 2, 256, 512),
    )
    new_weight_up = new_weight_up.reshape(2048, 512)
    new_weight_down = new_weight_down.reshape(4096, 256)
    return (
        new_weight_up,
        new_weight_down,
        new_moment_up,
        new_second_up,
        new_moment_down,
        new_second_down,
    )


def solution(mesh):
    devices = Mesh(mesh.devices.reshape(SIZES), AXES)
    columns = ("x", "y", "c")
    in_specs = (
        P("z", columns),
        P("z", columns),
        P("z", None, columns),
        P("z", None, columns),
        P(columns, None),
        P(columns, None),
        P("z", columns),
        P("z", columns),
        P(AXES, None),
        P(AXES, None),
    )
    out_specs = (
        P("z", columns),
        P("z", columns),
        P("z", columns),
        P("z", columns),
        P(AXES, None),
        P(AXES, None),
    )
    return jax.shard_map(
        per_device, mesh=devices, in_specs=in_specs, out_specs=out_specs, check_vma=False
    )
```

time: 819 us -> 147 us (0.18)
  waiting for transfers between devices: 682 us -> 40.4 us
  blocking collectives: 74.4 us -> 0 us
  starting transfers between devices: 0.17 us -> 57.4 us
  matrix products: 29.5 us -> 0 us
  Pallas kernels: 0 us -> 26.3 us
  between operations: 18.3 us -> 0.99 us
  local copies, waits for them, and re-layouts: 0.15 us -> 11.4 us
    reduce_scatter x2 -> x0, waiting for transfers between devices: 632 us -> none  [the longest x1 616 us: per_device(): lax.psum_scatter(jnp.dot(local_down, basis_down, preferred_element_type=j...]
    psum x1 -> x0, blocking collectives: 64.5 us -> none  [per_device(): lax.psum((local_sums[0], local_sums[1], local_sums[2], local_sums[3]), ('...]
    ppermute x0 -> x36, starting transfers between devices: none -> 49.8 us  [the longest x28 36.1 us: shift(): return lax.ppermute(value, AXES, shift_pairs(axis0, axis1, k))]
    all_gather x2 -> x0, waiting for transfers between devices: 49.2 us -> none  [the longest x1 41.5 us: per_device(): full_basis = lax.all_gather(basis_up, 'fsdp', axis=0, tiled=True)]
    ppermute x0 -> x36, waiting for transfers between devices: none -> 31.1 us  [the longest x28 24.3 us: shift(): return lax.ppermute(value, AXES, shift_pairs(axis0, axis1, k))]
    dot_general x4 -> x0, matrix products: 29.5 us -> none  [the longest x1 11.5 us: per_device(): jnp.dot(local_down, basis_down, preferred_element_type=jnp.float32)]
    pallas_call x0 -> x11, Pallas kernels: none -> 26.3 us  [the longest x2 10.5 us: project_up(): pl.pallas_call(project_up_kernel, out_shape=jax.ShapeDtypeStruct((256, 51...]
    all_gather x1 -> x0, blocking collectives: 9.87 us -> none  [per_device(): lax.all_gather(low_up, 'dp', axis=0, tiled=True)]
  transfers between devices with their start and end apart: 4 -> 37, of which waited for: 4 -> 10; matrix products, arithmetic and copies ran while one was open for 4% -> 8% of each run, Pallas kernels for 0% -> 12%
where the time goes in v1:
time: 147 us; the launch traced here: 146 us
  starting transfers between devices  57.4 us (39%)
  waiting for transfers between devices  40.4 us (27%)
  Pallas kernels  26.3 us (18%)
  local copies, waits for them, and re-layouts  11.4 us (8%)
  other arithmetic  9.85 us (7%)
    ppermute x28, starting transfers between devices, shift(): return lax.ppermute(value, AXES, shift_pairs(axis0, axis1, k))  36.1 us
    ppermute x28, waiting for transfers between devices, shift(): return lax.ppermute(value, AXES, shift_pairs(axis0, axis1, k))  24.3 us
    ppermute x8, starting transfers between devices, swap_cores(): return lax.ppermute(value, 'c', [(0, 1), (1, 0)])  13.6 us
    pallas_call x2, Pallas kernels, project_up(): pl.pallas_call(project_up_kernel, out_shape=jax.ShapeDtypeStruct((256, 51...  10.5 us
    all_to_all x1, waiting for transfers between devices, per_device(): sums = lax.all_to_all(sums, AXES, 0, 0, tiled=True)  9.32 us
    unnamed x36, local copies, waits for them, and re-layouts  8.24 us
    all_to_all x1, starting transfers between devices, per_device(): sums = lax.all_to_all(sums, AXES, 0, 0, tiled=True)  7.62 us
    pallas_call x6, Pallas kernels, project_rows(): pl.pallas_call(functools.partial(project_kernel, other is not None), out_...  7.31 us
  transfers between devices with their start and end apart: 37, of which 10 were waited for; matrix products, arithmetic and copies ran while one was open for 8% of the time, Pallas kernels for 12%

profile of v1, /device:TPU:1, one launch (start us, length us, event | category | flops | bytes accessed | tf_op | source)
XLA Modules:
  0.0 146.3 jit_solution(2223208864672705061)
XLA Ops:
  2.1 2.6 %collective-permute-start.3 = (bf16[256,256]{1,0:T(8,128)(2,1)}, bf16[256,256]{1,0:T(8,128)(2,1)S(1)}, u32[]{:S(2)}, u32[]{:S(2)}) collective-permute-start(bf16[256,256]{1,0:T(8,128)(2,1)} %param.14), channel_id=1, source_target_pairs={{0,24},{1,25},{2,26},{3,27},{4,28},{5,29},{6,30},{7,31},{8,0},{9,1... | collective-permute-start | bytes 393224 | tf_op jit(solution)/shard_map/ppermute | solution.py:48
  4.7 1.7 %collective-permute-start.2 = (bf16[256,256]{1,0:T(8,128)(2,1)}, bf16[256,256]{1,0:T(8,128)(2,1)S(1)}, u32[]{:S(2)}, u32[]{:S(2)}) collective-permute-start(bf16[256,256]{1,0:T(8,128)(2,1)} %param.14), channel_id=1, source_target_pairs={{0,16},{1,17},{2,18},{3,19},{4,20},{5,21},{6,22},{7,23},{8,24},{9,... | collective-permute-start | bytes 393224 | tf_op jit(solution)/shard_map/ppermute | solution.py:48
  6.5 3.4 %copy-done = bf16[1,16384,256]{2,1,0:T(8,128)(2,1)S(1)} copy-done((bf16[1,16384,256]{2,1,0:T(8,128)(2,1)S(1)}, bf16[1,16384,256]{2,1,0:T(8,128)(2,1)}, u32[]{:S(2)}) %copy-start) | copy-done | bytes 8388632
  11.9 1.8 %collective-permute-done.1 = bf16[256,256]{1,0:T(8,128)(2,1)S(1)} collective-permute-done((bf16[256,256]{1,0:T(8,128)(2,1)}, bf16[256,256]{1,0:T(8,128)(2,1)S(1)}, u32[]{:S(2)}, u32[]{:S(2)}) %collective-permute-start.1) | collective-permute-done | bytes 131104 | tf_op jit(solution)/shard_map/ppermute | solution.py:48
  13.8 2.4 %shard_map.146 = bf16[3,4,4,128,256]{4,3,2,1,0:T(8,128)(2,1)S(1)} custom-call(s32[4]{0:T(128)S(1)} %pad_add_fusion.place_ref, bf16[4,4,4,2,128,256]{5,4,3,2,1,0:T(8,128)(2,1)S(1)} %bitcast.67, bf16[4,4,4,2,128,256]{5,4,3,2,1,0:T(8,128)(2,1)S(1)} %bitcast.68, bf16[4,4,4,2,128,256]{5,4,3,2,1,0:T(8,128)(2,1)S(1)} %bitcast.69, ...), custom_call_target="tpu_custom_call" | custom-call | flops 3 | bytes 3 | tf_op jit(solution)/shard_map/pallas_call | solution.py:100
  17.6 6.7 %collective-permute-done.5.refs_5_ = bf16[1,4,4,128,256]{4,3,2,1,0:T(8,128)(2,1)S(1)} collective-permute-done((bf16[1,4,4,128,256]{4,3,2,1,0:T(8,128)(2,1)S(1)}, bf16[1,4,4,128,256]{4,3,2,1,0:T(8,128)(2,1)S(1)}, u32[]{:S(2)}, u32[]{:S(2)}) %collective-permute-start.5) | collective-permute-done | bytes 1048608 | tf_op jit(solution)/shard_map/ppermute | solution.py:52
  32.0 1.7 %multiply_reduce_fusion = f32[]{:T(128)} fusion(bf16[4096,256]{1,0:T(8,128)(2,1)S(1)} %copy-done.1), kind=kLoop, calls=%fused_computation | loop fusion | flops 3145727 | bytes 2097156 | tf_op jit(solution)/shard_map/reduce_sum | solution.py:320
  33.7 1.7 %multiply_reduce_fusion.1 = f32[]{:T(128)} fusion(bf16[2048,512]{1,0:T(8,128)(2,1)S(1)} %copy-done.2), kind=kLoop, calls=%fused_computation.1 | loop fusion | flops 3145727 | bytes 2097156 | tf_op jit(solution)/shard_map/reduce_sum | solution.py:319
  35.3 4.2 %collective-permute-done.9 = bf16[4,256,256]{2,1,0:T(8,128)(2,1)S(1)} collective-permute-done((bf16[4,256,256]{2,1,0:T(8,128)(2,1)S(1)}, bf16[4,256,256]{2,1,0:T(8,128)(2,1)S(1)}, u32[]{:S(2)}, u32[]{:S(2)}) %collective-permute-start.9) | collective-permute-done | bytes 524320 | tf_op jit(solution)/shard_map/ppermute | solution.py:48
  40.8 9.0 %collective-permute-done.8.refs_2_ = bf16[4,4,128,256]{3,2,1,0:T(8,128)(2,1)S(1)} collective-permute-done((bf16[4,4,128,256]{3,2,1,0:T(8,128)(2,1)S(1)}, bf16[4,4,128,256]{3,2,1,0:T(8,128)(2,1)S(1)}, u32[]{:S(2)}, u32[]{:S(2)}) %collective-permute-start.8) | collective-permute-done | bytes 1048608 | tf_op jit(solution)/shard_map/ppermute | solution.py:48
  49.8 2.2 %collective-permute-done.7.refs_1_ = bf16[4,4,128,256]{3,2,1,0:T(8,128)(2,1)S(1)} collective-permute-done((bf16[4,4,128,256]{3,2,1,0:T(8,128)(2,1)S(1)}, bf16[4,4,128,256]{3,2,1,0:T(8,128)(2,1)S(1)}, u32[]{:S(2)}, u32[]{:S(2)}) %collective-permute-start.7) | collective-permute-done | bytes 1048608 | tf_op jit(solution)/shard_map/ppermute | solution.py:48
  55.9 3.3 %collective-permute-start.13 = (bf16[4,128,256]{2,1,0:T(8,128)(2,1)S(1)}, bf16[4,128,256]{2,1,0:T(8,128)(2,1)S(1)}, u32[]{:S(2)}, u32[]{:S(2)}) collective-permute-start(bf16[4,128,256]{2,1,0:T(8,128)(2,1)S(1)} %get-tuple-element.30), channel_id=1, source_target_pairs={{0,16},{1,65},{2,18},{3,67},{4,20},{5,69},{6,22},{7,71},{8,24},{9,... | collective-permute-start | bytes 786440 | tf_op jit(solution)/shard_map/ppermute | solution.py:48
  60.3 1.6 %collective-permute-start.15 = (bf16[4,128,256]{2,1,0:T(8,128)(2,1)S(1)}, bf16[4,128,256]{2,1,0:T(8,128)(2,1)S(1)}, u32[]{:S(2)}, u32[]{:S(2)}) collective-permute-start(bf16[4,128,256]{2,1,0:T(8,128)(2,1)S(1)} %get-tuple-element.32), channel_id=1, source_target_pairs={{0,24},{1,97},{2,26},{3,99},{4,28},{5,101},{6,30},{7,103},{8,0},{9... | collective-permute-start | bytes 786440 | tf_op jit(solution)/shard_map/ppermute | solution.py:48
  63.6 2.5 %collective-permute-done.14 = bf16[4,128,256]{2,1,0:T(8,128)(2,1)S(1)} collective-permute-done((bf16[4,128,256]{2,1,0:T(8,128)(2,1)S(1)}, bf16[4,128,256]{2,1,0:T(8,128)(2,1)S(1)}, u32[]{:S(2)}, u32[]{:S(2)}) %collective-permute-start.14) | collective-permute-done | bytes 262176 | tf_op jit(solution)/shard_map/ppermute | solution.py:48
  67.1 2.6 %collective-permute-start.16 = (bf16[4,4,256,256]{3,2,1,0:T(8,128)(2,1)}, bf16[4,4,256,256]{3,2,1,0:T(8,128)(2,1)}, u32[]{:S(2)}, u32[]{:S(2)}) collective-permute-start(bf16[4,4,256,256]{3,2,1,0:T(8,128)(2,1)} %pad_maximum_fusion.basis_ref), channel_id=1, source_target_pairs={{0,1},{1,0},{2,3},{3,2},{4,5},{5,4},{6,7},{7,6},{8,9},{9,8},{10,11... | collective-permute-start | bytes 6291464 | tf_op jit(solution)/shard_map/ppermute | solution.py:52
  71.1 5.1 %shard_map.152.refs_8_ = f32[256,512]{1,0:T(8,128)} custom-call(s32[4]{0:T(128)} %copy-done.9, bf16[4,4,256,256]{3,2,1,0:T(8,128)(2,1)} %pad_maximum_fusion.basis_ref, bf16[8192,512]{1,0:T(8,128)(2,1)} %bitcast.95, bf16[8192,512]{1,0:T(8,128)(2,1)} %bitcast.96, bf16[8192,512]{1,0:T(8,128)(2,1)} %bitcast.97, bf16[8192,512]{1,0:T(8,128)(2,1)} %bitcast.98, ...), custom_call_target="tpu_custom_call" | custom-call | flops 1 | bytes 1 | tf_op jit(solution)/shard_map/pallas_call | solution.py:156
  77.0 1.7 %collective-permute-start.17 = (bf16[128,256]{1,0:T(8,128)(2,1)}, bf16[128,256]{1,0:T(8,128)(2,1)S(1)}, u32[]{:S(2)}, u32[]{:S(2)}) collective-permute-start(bf16[128,256]{1,0:T(8,128)(2,1)} %get-tuple-element.44), channel_id=1, source_target_pairs={{0,4},{1,5},{2,6},{3,7},{4,0},{5,1},{6,2},{7,3},{8,12},{9,13},{10,... | collective-permute-start | bytes 196616 | tf_op jit(solution)/shard_map/ppermute | solution.py:48
  79.1 2.3 %collective-permute-start.19 = (bf16[128,256]{1,0:T(8,128)(2,1)S(1)}, bf16[128,256]{1,0:T(8,128)(2,1)S(1)}, u32[]{:S(2)}, u32[]{:S(2)}) collective-permute-start(bf16[128,256]{1,0:T(8,128)(2,1)S(1)} %get-tuple-element.45), channel_id=1, source_target_pairs={{0,6},{1,7},{2,0},{3,1},{4,2},{5,3},{6,4},{7,5},{8,14},{9,15},{10,... | collective-permute-start | bytes 196616 | tf_op jit(solution)/shard_map/ppermute | solution.py:48
  82.5 5.3 %shard_map.153 = bf16[256,512]{1,0:T(8,128)(2,1)} custom-call(s32[4]{0:T(128)} %copy-done.9, bf16[4,4,256,256]{3,2,1,0:T(8,128)(2,1)} %collective-permute-done.16.basis_ref, bf16[8192,512]{1,0:T(8,128)(2,1)} %bitcast.103, bf16[8192,512]{1,0:T(8,128)(2,1)} %bitcast.104, bf16[8192,512]{1,0:T(8,128)(2,1)} %bitcast.105, bf16[8192,512]{1,0:T(8,128)(2,1)} %bitcast.106, ...), custom_call_target="tpu_custom_call" | custom-call | flops 1 | bytes 1 | tf_op jit(solution)/shard_map/pallas_call | solution.py:156
  88.7 1.6 %collective-permute-start.21 = (bf16[128,256]{1,0:T(8,128)(2,1)S(1)}, bf16[128,256]{1,0:T(8,128)(2,1)S(1)}, u32[]{:S(2)}, u32[]{:S(2)}) collective-permute-start(bf16[128,256]{1,0:T(8,128)(2,1)S(1)} %get-tuple-element.41), channel_id=1, source_target_pairs={{0,4},{1,17},{2,6},{3,19},{4,0},{5,21},{6,2},{7,23},{8,12},{9,25},... | collective-permute-start | bytes 196616 | tf_op jit(solution)/shard_map/ppermute | solution.py:48
  91.2 2.3 %collective-permute-start.26 = (bf16[64,512]{1,0:T(8,128)(2,1)S(1)}, bf16[64,512]{1,0:T(8,128)(2,1)S(1)}, u32[]{:S(2)}, u32[]{:S(2)}) collective-permute-start(bf16[64,512]{1,0:T(8,128)(2,1)S(1)} %get-tuple-element.54), channel_id=1, source_target_pairs={{0,64},{1,65},{2,66},{3,67},{4,68},{5,69},{6,70},{7,71},{8,72},{9,... | collective-permute-start | bytes 196616 | tf_op jit(solution)/shard_map/ppermute | solution.py:48
  94.3 1.9 %collective-permute-start.28 = (bf16[64,512]{1,0:T(8,128)(2,1)S(1)}, bf16[64,512]{1,0:T(8,128)(2,1)S(1)}, u32[]{:S(2)}, u32[]{:S(2)}) collective-permute-start(bf16[64,512]{1,0:T(8,128)(2,1)S(1)} %get-tuple-element.55), channel_id=1, source_target_pairs={{0,96},{1,97},{2,98},{3,99},{4,100},{5,101},{6,102},{7,103},{8,104... | collective-permute-start | bytes 196616 | tf_op jit(solution)/shard_map/ppermute | solution.py:48
  98.4 1.7 %divide_convert_fusion = (bf16[64,512]{1,0:T(8,128)(2,1)S(1)}, f32[64,512]{1,0:T(8,128)}, f32[64,512]{1,0:T(8,128)}) fusion(bf16[64,512]{1,0:T(8,128)(2,1)S(1)} %collective-permute-done.28, bf16[64,512]{1,0:T(8,128)(2,1)S(1)} %collective-permute-done.27, bf16[64,512]{1,0:T(8,128)(2,1)S(1)} %collective-permute-done.26, bf16[4,64,512]{2,1,0:T(8,128)(2,1)} %bitcast.114, ...), kind=kLoop, calls=%fused_computation.13 | loop fusion | flops 655360 | bytes 851972 | tf_op jit(solution)/shard_map/convert_element_type | solution.py:30
  100.1 3.3 %collective-permute-start.30 = (bf16[64,512]{1,0:T(8,128)(2,1)S(1)}, bf16[64,512]{1,0:T(8,128)(2,1)S(1)}, u32[]{:S(2)}, u32[]{:S(2)}) collective-permute-start(bf16[64,512]{1,0:T(8,128)(2,1)S(1)} %get-tuple-element.38), channel_id=1, source_target_pairs={{0,64},{1,65},{2,66},{3,67},{4,68},{5,69},{6,70},{7,71},{8,72},{9,... | collective-permute-start | bytes 196616 | tf_op jit(solution)/shard_map/ppermute | solution.py:48
  103.6 1.8 %collective-permute-start.24 = (bf16[4,128,256]{2,1,0:T(8,128)(2,1)S(1)}, bf16[4,128,256]{2,1,0:T(8,128)(2,1)}, u32[]{:S(2)}, u32[]{:S(2)}) collective-permute-start(bf16[4,128,256]{2,1,0:T(8,128)(2,1)S(1)} %pad_maximum_fusion.2.refs_0_), channel_id=1, source_target_pairs={{0,16},{1,5},{2,18},{3,7},{4,20},{5,1},{6,22},{7,3},{8,24},{9,13},... | collective-permute-start | bytes 786440 | tf_op jit(solution)/shard_map/ppermute | solution.py:48
  106.3 3.5 %collective-permute-start.32 = (bf16[4,128,256]{2,1,0:T(8,128)(2,1)S(1)}, bf16[4,128,256]{2,1,0:T(8,128)(2,1)}, u32[]{:S(2)}, u32[]{:S(2)}) collective-permute-start(bf16[4,128,256]{2,1,0:T(8,128)(2,1)S(1)} %pad_maximum_fusion.2.refs_0_), channel_id=1, source_target_pairs={{0,1},{1,0},{2,3},{3,2},{4,5},{5,4},{6,7},{7,6},{8,9},{9,8},{10,11... | collective-permute-start | bytes 786440 | tf_op jit(solution)/shard_map/ppermute | solution.py:52
  109.9 3.3 %collective-permute-done.23.refs_1_ = bf16[4,128,256]{2,1,0:T(8,128)(2,1)} collective-permute-done((bf16[4,128,256]{2,1,0:T(8,128)(2,1)S(1)}, bf16[4,128,256]{2,1,0:T(8,128)(2,1)}, u32[]{:S(2)}, u32[]{:S(2)}) %collective-permute-start.23) | collective-permute-done | bytes 262176 | tf_op jit(solution)/shard_map/ppermute | solution.py:48
  113.2 3.8 %collective-permute-start.33 = (bf16[4,128,256]{2,1,0:T(8,128)(2,1)}, bf16[4,128,256]{2,1,0:T(8,128)(2,1)}, u32[]{:S(2)}, u32[]{:S(2)}) collective-permute-start(bf16[4,128,256]{2,1,0:T(8,128)(2,1)} %collective-permute-done.23.refs_1_), channel_id=1, source_target_pairs={{0,1},{1,0},{2,3},{3,2},{4,5},{5,4},{6,7},{7,6},{8,9},{9,8},{10,11... | collective-permute-start | bytes 786440 | tf_op jit(solution)/shard_map/ppermute | solution.py:52
  118.0 2.5 %shard_map.154 = f32[128,1,128]{2,1,0:T(1,128)S(1)} custom-call(f32[2]{0:T(128)S(1)} %pad_maximum_fusion.5.weights_ref, bf16[4,128,256]{2,1,0:T(8,128)(2,1)S(1)} %pad_maximum_fusion.2.refs_0_, bf16[4,128,256]{2,1,0:T(8,128)(2,1)} %collective-permute-done.23.refs_1_, bf16[4,128,256]{2,1,0:T(8,128)(2,1)} %collective-permute-done.24.refs_2_, ...), custom_call_target="tpu_custom_call" | custom-call | flops 17179869184 | bytes 3145728 | tf_op jit(solution)/shard_map/pallas_call | solution.py:228
  121.8 7.6 %all-to-all-start = ((f32[128,1,128]{2,1,0:T(1,128)}), f32[128,1,128]{2,1,0:T(1,128)}, u32[]{:S(2)}, u32[]{:S(2)}) async-start(f32[128,1,128]{2,1,0:T(1,128)} %copy-done.8), calls=%async_computation | async-start | bytes 131072 | tf_op jit(solution)/shard_map/all_to_all | solution.py:390
  129.4 9.3 %all-to-all-done.sums_ref = f32[128,1,128]{2,1,0:T(1,128)} async-done(((f32[128,1,128]{2,1,0:T(1,128)}), f32[128,1,128]{2,1,0:T(1,128)}, u32[]{:S(2)}, u32[]{:S(2)}) %all-to-all-start) | async-done | bytes 65568 | tf_op jit(solution)/shard_map/all_to_all | solution.py:390
  141.3 5.0 %shard_map.155 = (bf16[4,2,256,512]{3,2,1,0:T(8,128)(2,1)}, bf16[4,4,2,128,256]{4,3,2,1,0:T(8,128)(2,1)}) custom-call(s32[4]{0:T(128)S(1)} %copy-done.10, f32[128,1,128]{2,1,0:T(1,128)} %all-to-all-done.sums_ref, bf16[4,128,256]{2,1,0:T(8,128)(2,1)S(1)} %pad_maximum_fusion.2.refs_0_, bf16[4,128,256]{2,1,0:T(8,128)(2,1)} %collective-permute-done.23.refs_1_, ...), custom_call_target="tpu_custom_call" | custom-call | flops 1073741824 | bytes 11534336 | tf_op jit(solution)/shard_map/pallas_call | solution.py:274
  (108 shorter events, 35.8 us)
Async XLA Ops:
  2.1 9.7 %collective-permute-start.3 = (bf16[256,256]{1,0:T(8,128)(2,1)}, bf16[256,256]{1,0:T(8,128)(2,1)S(1)}, u32[]{:S(2)}, u32[]{:S(2)}) collective-permute-start(bf16[256,256]{1,0:T(8,128)(2,1)} %param.14), channel_id=1, source_target_pairs={{0,24},{1,25},{2,26},{3,27},{4,28},{5,29},{6,30},{7,31},{8,0},{9,1... | collective-permute-start | bytes 393224 | tf_op jit(solution)/shard_map/ppermute | solution.py:48
  4.7 9.0 %collective-permute-start.1 = (bf16[256,256]{1,0:T(8,128)(2,1)}, bf16[256,256]{1,0:T(8,128)(2,1)S(1)}, u32[]{:S(2)}, u32[]{:S(2)}) collective-permute-start(bf16[256,256]{1,0:T(8,128)(2,1)} %param.14), channel_id=1, source_target_pairs={{0,8},{1,9},{2,10},{3,11},{4,12},{5,13},{6,14},{7,15},{8,16},{9,17... | collective-permute-start | bytes 393224 | tf_op jit(solution)/shard_map/ppermute | solution.py:48
  4.7 9.0 %collective-permute-start.2 = (bf16[256,256]{1,0:T(8,128)(2,1)}, bf16[256,256]{1,0:T(8,128)(2,1)S(1)}, u32[]{:S(2)}, u32[]{:S(2)}) collective-permute-start(bf16[256,256]{1,0:T(8,128)(2,1)} %param.14), channel_id=1, source_target_pairs={{0,16},{1,17},{2,18},{3,19},{4,20},{5,21},{6,22},{7,23},{8,24},{9,... | collective-permute-start | bytes 393224 | tf_op jit(solution)/shard_map/ppermute | solution.py:48
  16.2 9.4 %collective-permute-start.4 = (bf16[3,4,4,128,256]{4,3,2,1,0:T(8,128)(2,1)S(1)}, bf16[3,4,4,128,256]{4,3,2,1,0:T(8,128)(2,1)S(1)}, u32[]{:S(2)}, u32[]{:S(2)}) collective-permute-start(bf16[3,4,4,128,256]{4,3,2,1,0:T(8,128)(2,1)S(1)} %shard_map.146), channel_id=1, source_target_pairs={{0,1},{1,0},{2,3},{3,2},{4,5},{5,4},{6,7},{7,6},{8,9},{9,8},{10,11... | collective-permute-start | bytes 9437192 | tf_op jit(solution)/shard_map/ppermute | solution.py:52
  17.5 6.8 %collective-permute-start.5 = (bf16[1,4,4,128,256]{4,3,2,1,0:T(8,128)(2,1)S(1)}, bf16[1,4,4,128,256]{4,3,2,1,0:T(8,128)(2,1)S(1)}, u32[]{:S(2)}, u32[]{:S(2)}) collective-permute-start(bf16[1,4,4,128,256]{4,3,2,1,0:T(8,128)(2,1)S(1)} %shard_map.145), channel_id=1, source_target_pairs={{0,1},{1,0},{2,3},{3,2},{4,5},{5,4},{6,7},{7,6},{8,9},{9,8},{10,11... | collective-permute-start | bytes 3145736 | tf_op jit(solution)/shard_map/ppermute | solution.py:52
  25.2 15.6 %collective-permute-start.6 = (bf16[4,4,128,256]{3,2,1,0:T(8,128)(2,1)S(1)}, bf16[4,4,128,256]{3,2,1,0:T(8,128)(2,1)S(1)}, u32[]{:S(2)}, u32[]{:S(2)}) collective-permute-start(bf16[4,4,128,256]{3,2,1,0:T(8,128)(2,1)S(1)} %bitcast.90), channel_id=1, source_target_pairs={{0,64},{1,17},{2,66},{3,19},{4,68},{5,21},{6,70},{7,23},{8,72},{9,... | collective-permute-start | bytes 3145736 | tf_op jit(solution)/shard_map/ppermute | solution.py:48
  27.6 22.2 %collective-permute-start.8 = (bf16[4,4,128,256]{3,2,1,0:T(8,128)(2,1)S(1)}, bf16[4,4,128,256]{3,2,1,0:T(8,128)(2,1)S(1)}, u32[]{:S(2)}, u32[]{:S(2)}) collective-permute-start(bf16[4,4,128,256]{3,2,1,0:T(8,128)(2,1)S(1)} %bitcast.92), channel_id=1, source_target_pairs={{0,96},{1,25},{2,98},{3,27},{4,100},{5,29},{6,102},{7,31},{8,104},... | collective-permute-start | bytes 3145736 | tf_op jit(solution)/shard_map/ppermute | solution.py:48
  29.2 22.8 %collective-permute-start.7 = (bf16[4,4,128,256]{3,2,1,0:T(8,128)(2,1)S(1)}, bf16[4,4,128,256]{3,2,1,0:T(8,128)(2,1)S(1)}, u32[]{:S(2)}, u32[]{:S(2)}) collective-permute-start(bf16[4,4,128,256]{3,2,1,0:T(8,128)(2,1)S(1)} %bitcast.91), channel_id=1, source_target_pairs={{0,32},{1,9},{2,34},{3,11},{4,36},{5,13},{6,38},{7,15},{8,40},{9,1... | collective-permute-start | bytes 3145736 | tf_op jit(solution)/shard_map/ppermute | solution.py:48
  29.2 10.3 %collective-permute-start.9 = (bf16[4,256,256]{2,1,0:T(8,128)(2,1)S(1)}, bf16[4,256,256]{2,1,0:T(8,128)(2,1)S(1)}, u32[]{:S(2)}, u32[]{:S(2)}) collective-permute-start(bf16[4,256,256]{2,1,0:T(8,128)(2,1)S(1)} %get-tuple-element.49), channel_id=1, source_target_pairs={{0,2},{1,3},{2,4},{3,5},{4,6},{5,7},{6,0},{7,1},{8,10},{9,11},{10,... | collective-permute-start | bytes 1572872 | tf_op jit(solution)/shard_map/ppermute | solution.py:48
  30.5 9.1 %collective-permute-start.11 = (bf16[4,256,256]{2,1,0:T(8,128)(2,1)S(1)}, bf16[4,256,256]{2,1,0:T(8,128)(2,1)S(1)}, u32[]{:S(2)}, u32[]{:S(2)}) collective-permute-start(bf16[4,256,256]{2,1,0:T(8,128)(2,1)S(1)} %get-tuple-element.49), channel_id=1, source_target_pairs={{0,6},{1,7},{2,0},{3,1},{4,2},{5,3},{6,4},{7,5},{8,14},{9,15},{10,... | collective-permute-start | bytes 1572872 | tf_op jit(solution)/shard_map/ppermute | solution.py:48
  53.1 8.9 %collective-permute-start.10 = (bf16[2,256,256]{2,1,0:T(8,128)(2,1)S(1)}, bf16[2,256,256]{2,1,0:T(8,128)(2,1)S(1)}, u32[]{:S(2)}, u32[]{:S(2)}) collective-permute-start(bf16[2,256,256]{2,1,0:T(8,128)(2,1)S(1)} %slice.8), channel_id=1, source_target_pairs={{0,2},{1,3},{2,4},{3,5},{4,6},{5,7},{6,0},{7,1},{8,10},{9,11},{10,... | collective-permute-start | bytes 786440 | tf_op jit(solution)/shard_map/ppermute | solution.py:48
  54.4 7.5 %collective-permute-start.12 = (bf16[2,256,256]{2,1,0:T(8,128)(2,1)S(1)}, bf16[2,256,256]{2,1,0:T(8,128)(2,1)S(1)}, u32[]{:S(2)}, u32[]{:S(2)}) collective-permute-start(bf16[2,256,256]{2,1,0:T(8,128)(2,1)S(1)} %slice.9), channel_id=1, source_target_pairs={{0,6},{1,7},{2,0},{3,1},{4,2},{5,3},{6,4},{7,5},{8,14},{9,15},{10,... | collective-permute-start | bytes 786440 | tf_op jit(solution)/shard_map/ppermute | solution.py:48
  55.9 7.6 %collective-permute-start.13 = (bf16[4,128,256]{2,1,0:T(8,128)(2,1)S(1)}, bf16[4,128,256]{2,1,0:T(8,128)(2,1)S(1)}, u32[]{:S(2)}, u32[]{:S(2)}) collective-permute-start(bf16[4,128,256]{2,1,0:T(8,128)(2,1)S(1)} %get-tuple-element.30), channel_id=1, source_target_pairs={{0,16},{1,65},{2,18},{3,67},{4,20},{5,69},{6,22},{7,71},{8,24},{9,... | collective-permute-start | bytes 786440 | tf_op jit(solution)/shard_map/ppermute | solution.py:48
  59.3 6.9 %collective-permute-start.14 = (bf16[4,128,256]{2,1,0:T(8,128)(2,1)S(1)}, bf16[4,128,256]{2,1,0:T(8,128)(2,1)S(1)}, u32[]{:S(2)}, u32[]{:S(2)}) collective-permute-start(bf16[4,128,256]{2,1,0:T(8,128)(2,1)S(1)} %get-tuple-element.31), channel_id=1, source_target_pairs={{0,8},{1,33},{2,10},{3,35},{4,12},{5,37},{6,14},{7,39},{8,16},{9,4... | collective-permute-start | bytes 786440 | tf_op jit(solution)/shard_map/ppermute | solution.py:48
  60.3 6.9 %collective-permute-start.15 = (bf16[4,128,256]{2,1,0:T(8,128)(2,1)S(1)}, bf16[4,128,256]{2,1,0:T(8,128)(2,1)S(1)}, u32[]{:S(2)}, u32[]{:S(2)}) collective-permute-start(bf16[4,128,256]{2,1,0:T(8,128)(2,1)S(1)} %get-tuple-element.32), channel_id=1, source_target_pairs={{0,24},{1,97},{2,26},{3,99},{4,28},{5,101},{6,30},{7,103},{8,0},{9... | collective-permute-start | bytes 786440 | tf_op jit(solution)/shard_map/ppermute | solution.py:48
  67.1 15.3 %collective-permute-start.16 = (bf16[4,4,256,256]{3,2,1,0:T(8,128)(2,1)}, bf16[4,4,256,256]{3,2,1,0:T(8,128)(2,1)}, u32[]{:S(2)}, u32[]{:S(2)}) collective-permute-start(bf16[4,4,256,256]{3,2,1,0:T(8,128)(2,1)} %pad_maximum_fusion.basis_ref), channel_id=1, source_target_pairs={{0,1},{1,0},{2,3},{3,2},{4,5},{5,4},{6,7},{7,6},{8,9},{9,8},{10,11... | collective-permute-start | bytes 6291464 | tf_op jit(solution)/shard_map/ppermute | solution.py:52
  77.0 10.8 %collective-permute-start.17 = (bf16[128,256]{1,0:T(8,128)(2,1)}, bf16[128,256]{1,0:T(8,128)(2,1)S(1)}, u32[]{:S(2)}, u32[]{:S(2)}) collective-permute-start(bf16[128,256]{1,0:T(8,128)(2,1)} %get-tuple-element.44), channel_id=1, source_target_pairs={{0,4},{1,5},{2,6},{3,7},{4,0},{5,1},{6,2},{7,3},{8,12},{9,13},{10,... | collective-permute-start | bytes 196616 | tf_op jit(solution)/shard_map/ppermute | solution.py:48
  78.7 9.2 %collective-permute-start.18 = (bf16[128,256]{1,0:T(8,128)(2,1)}, bf16[128,256]{1,0:T(8,128)(2,1)S(1)}, u32[]{:S(2)}, u32[]{:S(2)}) collective-permute-start(bf16[128,256]{1,0:T(8,128)(2,1)} %get-tuple-element.46), channel_id=1, source_target_pairs={{0,2},{1,3},{2,4},{3,5},{4,6},{5,7},{6,0},{7,1},{8,10},{9,11},{10,... | collective-permute-start | bytes 196616 | tf_op jit(solution)/shard_map/ppermute | solution.py:48
  79.1 8.8 %collective-permute-start.19 = (bf16[128,256]{1,0:T(8,128)(2,1)S(1)}, bf16[128,256]{1,0:T(8,128)(2,1)S(1)}, u32[]{:S(2)}, u32[]{:S(2)}) collective-permute-start(bf16[128,256]{1,0:T(8,128)(2,1)S(1)} %get-tuple-element.45), channel_id=1, source_target_pairs={{0,6},{1,7},{2,0},{3,1},{4,2},{5,3},{6,4},{7,5},{8,14},{9,15},{10,... | collective-permute-start | bytes 196616 | tf_op jit(solution)/shard_map/ppermute | solution.py:48
  88.7 14.7 %collective-permute-start.20 = (bf16[128,256]{1,0:T(8,128)(2,1)S(1)}, bf16[128,256]{1,0:T(8,128)(2,1)S(1)}, u32[]{:S(2)}, u32[]{:S(2)}) collective-permute-start(bf16[128,256]{1,0:T(8,128)(2,1)S(1)} %get-tuple-element.41), channel_id=1, source_target_pairs={{0,2},{1,9},{2,4},{3,11},{4,6},{5,13},{6,0},{7,15},{8,10},{9,17},{... | collective-permute-start | bytes 196616 | tf_op jit(solution)/shard_map/ppermute | solution.py:48
  88.7 14.8 %collective-permute-start.21 = (bf16[128,256]{1,0:T(8,128)(2,1)S(1)}, bf16[128,256]{1,0:T(8,128)(2,1)S(1)}, u32[]{:S(2)}, u32[]{:S(2)}) collective-permute-start(bf16[128,256]{1,0:T(8,128)(2,1)S(1)} %get-tuple-element.41), channel_id=1, source_target_pairs={{0,4},{1,17},{2,6},{3,19},{4,0},{5,21},{6,2},{7,23},{8,12},{9,25},... | collective-permute-start | bytes 196616 | tf_op jit(solution)/shard_map/ppermute | solution.py:48
  97.3 6.2 %collective-permute-start.22 = (bf16[128,256]{1,0:T(8,128)(2,1)S(1)}, bf16[128,256]{1,0:T(8,128)(2,1)S(1)}, u32[]{:S(2)}, u32[]{:S(2)}) collective-permute-start(bf16[128,256]{1,0:T(8,128)(2,1)S(1)} %get-tuple-element.41), channel_id=1, source_target_pairs={{0,6},{1,25},{2,0},{3,27},{4,2},{5,29},{6,4},{7,31},{8,14},{9,1},{... | collective-permute-start | bytes 196616 | tf_op jit(solution)/shard_map/ppermute | solution.py:48
  100.1 6.2 %collective-permute-start.30 = (bf16[64,512]{1,0:T(8,128)(2,1)S(1)}, bf16[64,512]{1,0:T(8,128)(2,1)S(1)}, u32[]{:S(2)}, u32[]{:S(2)}) collective-permute-start(bf16[64,512]{1,0:T(8,128)(2,1)S(1)} %get-tuple-element.38), channel_id=1, source_target_pairs={{0,64},{1,65},{2,66},{3,67},{4,68},{5,69},{6,70},{7,71},{8,72},{9,... | collective-permute-start | bytes 196616 | tf_op jit(solution)/shard_map/ppermute | solution.py:48
  103.4 6.4 %collective-permute-start.31 = (bf16[64,512]{1,0:T(8,128)(2,1)S(1)}, bf16[64,512]{1,0:T(8,128)(2,1)S(1)}, u32[]{:S(2)}, u32[]{:S(2)}) collective-permute-start(bf16[64,512]{1,0:T(8,128)(2,1)S(1)} %get-tuple-element.38), channel_id=1, source_target_pairs={{0,96},{1,97},{2,98},{3,99},{4,100},{5,101},{6,102},{7,103},{8,104... | collective-permute-start | bytes 196616 | tf_op jit(solution)/shard_map/ppermute | solution.py:48
  103.5 9.7 %collective-permute-start.23 = (bf16[4,128,256]{2,1,0:T(8,128)(2,1)S(1)}, bf16[4,128,256]{2,1,0:T(8,128)(2,1)}, u32[]{:S(2)}, u32[]{:S(2)}) collective-permute-start(bf16[4,128,256]{2,1,0:T(8,128)(2,1)S(1)} %pad_maximum_fusion.2.refs_0_), channel_id=1, source_target_pairs={{0,8},{1,3},{2,10},{3,5},{4,12},{5,7},{6,14},{7,1},{8,16},{9,11},{... | collective-permute-start | bytes 786440 | tf_op jit(solution)/shard_map/ppermute | solution.py:48
  103.6 13.4 %collective-permute-start.24 = (bf16[4,128,256]{2,1,0:T(8,128)(2,1)S(1)}, bf16[4,128,256]{2,1,0:T(8,128)(2,1)}, u32[]{:S(2)}, u32[]{:S(2)}) collective-permute-start(bf16[4,128,256]{2,1,0:T(8,128)(2,1)S(1)} %pad_maximum_fusion.2.refs_0_), channel_id=1, source_target_pairs={{0,16},{1,5},{2,18},{3,7},{4,20},{5,1},{6,22},{7,3},{8,24},{9,13},... | collective-permute-start | bytes 786440 | tf_op jit(solution)/shard_map/ppermute | solution.py:48
  105.4 11.7 %collective-permute-start.25 = (bf16[4,128,256]{2,1,0:T(8,128)(2,1)S(1)}, bf16[4,128,256]{2,1,0:T(8,128)(2,1)}, u32[]{:S(2)}, u32[]{:S(2)}) collective-permute-start(bf16[4,128,256]{2,1,0:T(8,128)(2,1)S(1)} %pad_maximum_fusion.2.refs_0_), channel_id=1, source_target_pairs={{0,24},{1,7},{2,26},{3,1},{4,28},{5,3},{6,30},{7,5},{8,0},{9,15},{... | collective-permute-start | bytes 786440 | tf_op jit(solution)/shard_map/ppermute | solution.py:48
  106.3 23.1 %collective-permute-start.32 = (bf16[4,128,256]{2,1,0:T(8,128)(2,1)S(1)}, bf16[4,128,256]{2,1,0:T(8,128)(2,1)}, u32[]{:S(2)}, u32[]{:S(2)}) collective-permute-start(bf16[4,128,256]{2,1,0:T(8,128)(2,1)S(1)} %pad_maximum_fusion.2.refs_0_), channel_id=1, source_target_pairs={{0,1},{1,0},{2,3},{3,2},{4,5},{5,4},{6,7},{7,6},{8,9},{9,8},{10,11... | collective-permute-start | bytes 786440 | tf_op jit(solution)/shard_map/ppermute | solution.py:52
  113.2 25.5 %collective-permute-start.33 = (bf16[4,128,256]{2,1,0:T(8,128)(2,1)}, bf16[4,128,256]{2,1,0:T(8,128)(2,1)}, u32[]{:S(2)}, u32[]{:S(2)}) collective-permute-start(bf16[4,128,256]{2,1,0:T(8,128)(2,1)} %collective-permute-done.23.refs_1_), channel_id=1, source_target_pairs={{0,1},{1,0},{2,3},{3,2},{4,5},{5,4},{6,7},{7,6},{8,9},{9,8},{10,11... | collective-permute-start | bytes 786440 | tf_op jit(solution)/shard_map/ppermute | solution.py:52
  117.0 21.7 %collective-permute-start.34 = (bf16[4,128,256]{2,1,0:T(8,128)(2,1)}, bf16[4,128,256]{2,1,0:T(8,128)(2,1)}, u32[]{:S(2)}, u32[]{:S(2)}) collective-permute-start(bf16[4,128,256]{2,1,0:T(8,128)(2,1)} %collective-permute-done.24.refs_2_), channel_id=1, source_target_pairs={{0,1},{1,0},{2,3},{3,2},{4,5},{5,4},{6,7},{7,6},{8,9},{9,8},{10,11... | collective-permute-start | bytes 786440 | tf_op jit(solution)/shard_map/ppermute | solution.py:52
  117.1 21.7 %collective-permute-start.35 = (bf16[4,128,256]{2,1,0:T(8,128)(2,1)}, bf16[4,128,256]{2,1,0:T(8,128)(2,1)}, u32[]{:S(2)}, u32[]{:S(2)}) collective-permute-start(bf16[4,128,256]{2,1,0:T(8,128)(2,1)} %collective-permute-done.25.refs_3_), channel_id=1, source_target_pairs={{0,1},{1,0},{2,3},{3,2},{4,5},{5,4},{6,7},{7,6},{8,9},{9,8},{10,11... | collective-permute-start | bytes 786440 | tf_op jit(solution)/shard_map/ppermute | solution.py:52
  121.8 17.0 %all-to-all-start = ((f32[128,1,128]{2,1,0:T(1,128)}), f32[128,1,128]{2,1,0:T(1,128)}, u32[]{:S(2)}, u32[]{:S(2)}) async-start(f32[128,1,128]{2,1,0:T(1,128)} %copy-done.8), calls=%async_computation | async-start | bytes 131072 | tf_op jit(solution)/shard_map/all_to_all | solution.py:390
  (23 other events, 185.1 us)

commit v2 on v1

--- a/solution.py
+++ b/solution.py
@@ -50,6 +50,10 @@
 
 def swap_cores(value):
     return lax.ppermute(value, "c", [(0, 1), (1, 0)])
+
+
+def exchange(value, mask):
+    return lax.ppermute(value, "z", [(i, i ^ mask) for i in range(4)])
 
 
 def pick(stacked, index):
@@ -239,17 +243,18 @@
 
 def update_kernel(place_ref, sums_ref, *refs):
     low_refs, (basis_down_ref, weight_down_ref) = refs[:8], refs[8:10]
-    own_ref, other_ref, low_up_ref, weight_up_ref, up_ref, down_ref = refs[10:]
+    own_ref, other_ref, low_up_hbm, weight_up_hbm, up_hbm, down_hbm = refs[10:16]
+    low_up_ref, weight_up_ref, up_ref, down_ref, in_sems, out_sems = refs[16:]
+    loads = [
+        pltpu.make_async_copy(low_up_hbm, low_up_ref, in_sems.at[0]),
+        pltpu.make_async_copy(weight_up_hbm, weight_up_ref, in_sems.at[1]),
+    ]
+    for copy in loads:
+        copy.start()
     sums = jnp.sum(sums_ref[...], axis=0)
     scale_up = learn_rate * (jnp.sqrt(sums[:, 0:1]) / (jnp.sqrt(sums[:, 2:3]) + norm_eps))
     scale_down = learn_rate * (jnp.sqrt(sums[:, 1:2]) / (jnp.sqrt(sums[:, 3:4]) + norm_eps))
     core0 = place_ref[2]
-    for back in range(4):
-        y = (place_ref[3] + 4 - back) % 4
-        for basis_ref, core in ((own_ref, core0), (other_ref, 1 - core0)):
-            delta = jnp.dot(basis_ref[back], low_up_ref[...], preferred_element_type=f32)
-            old = weight_up_ref[y, core].astype(f32)
-            up_ref[y, core] = (old - scale_up * delta).astype(bf16)
     for i, low_ref in enumerate(low_refs):
         outer = i % 4
         core = core0 if i < 4 else 1 - core0
@@ -266,10 +271,25 @@
             down_ref[x, y, core] = (
                 old - scale_down * delta[inner * 128 : (inner + 1) * 128]
             ).astype(bf16)
+    stores = [pltpu.make_async_copy(down_ref, down_hbm, out_sems.at[4])]
+    stores[0].start()
+    for copy in loads:
+        copy.wait()
+    for y in range(4):
+        back = (place_ref[3] + 4 - y) % 4
+        for basis_ref, core in ((own_ref, core0), (other_ref, 1 - core0)):
+            delta = jnp.dot(basis_ref[back], low_up_ref[...], preferred_element_type=f32)
+            old = weight_up_ref[y, core].astype(f32)
+            up_ref[y, core] = (old - scale_up * delta).astype(bf16)
+        stores.append(pltpu.make_async_copy(up_ref.at[y], up_hbm.at[y], out_sems.at[y]))
+        stores[-1].start()
+    for copy in stores:
+        copy.wait()
 
 
 def update(place, sums, lows, basis_down, weight_down, own, other, low_up, weight_up):
     vmem = pl.BlockSpec(memory_space=pltpu.VMEM)
+    hbm = pl.BlockSpec(memory_space=pltpu.HBM)
     operands = [place, sums, *lows, basis_down, weight_down, own, other, low_up, weight_up]
     return pl.pallas_call(
         update_kernel,
@@ -277,9 +297,17 @@
             jax.ShapeDtypeStruct(weight_up.shape, bf16),
             jax.ShapeDtypeStruct(weight_down.shape, bf16),
         ],
-        in_specs=[pl.BlockSpec(memory_space=pltpu.SMEM)] + [vmem] * (len(operands) - 1),
-        out_specs=[vmem, vmem],
-        compiler_params=pltpu.CompilerParams(vmem_limit_bytes=16 << 20),
+        in_specs=[pl.BlockSpec(memory_space=pltpu.SMEM)] + [vmem] * (len(operands) - 3) + [hbm] * 2,
+        out_specs=[hbm, hbm],
+        scratch_shapes=[
+            pltpu.VMEM(low_up.shape, bf16),
+            pltpu.VMEM(weight_up.shape, bf16),
+            pltpu.VMEM(weight_up.shape, bf16),
+            pltpu.VMEM(weight_down.shape, bf16),
+            pltpu.SemaphoreType.DMA((2,)),
+            pltpu.SemaphoreType.DMA((5,)),
+        ],
+        compiler_params=pltpu.CompilerParams(vmem_limit_bytes=24 << 20),
         cost_estimate=pl.CostEstimate(
             flops=4 * 2048 * 256 * 512, bytes_accessed=11 << 20, transcendentals=0
         ),
@@ -319,15 +347,13 @@
     wsq_up = jnp.sum(weight_upf * weight_upf)
     wsq_down = jnp.sum(weight_downf * weight_downf)
 
-    other_basis_down = swap_cores(basis_down)
-    place = after(place, other_basis_down)
     half = functools.partial(project_rows, place, local_down, basis_down, False)
     whole = functools.partial(project_rows, place, local_down, basis_down, True)
     half_2 = half((2,))
     got_2 = swap_cores(half_2)
     ready = {2: whole((2,), got_2)[0]}
     half_130 = project_rows(
-        after(place, half_2, near), local_down, basis_down, False, (1, 3, 0)
+        after(place, ready[2], near), local_down, basis_down, False, (1, 3, 0)
     )
     got_130 = swap_cores(half_130)
     ready[1] = whole((1,), got_130, 0)[0]
@@ -339,16 +365,21 @@
     two = [two_own] + [shift(t, "x", "z", k) for t, k in zip(two, (2, 1, 3))]
 
     back, ahead = shift(near, "y", "y", 1), shift(near, "y", "y", 3)
-    back_half, ahead_half = after(back[:2], two[0]), after(ahead[2:], two[0])
+    back_half, ahead_half = after(back[:2], ready[0]), after(ahead[2:], ready[0])
     far = jnp.concatenate([shift(back_half, "y", "y", 1), shift(ahead_half, "y", "y", 3)])
-    own_basis = jnp.stack([near, back, far, ahead])
-    own_basis = after(own_basis, *two[1:])
+    own_basis = jnp.stack([after(near, two_own), back, far, ahead])
     other_basis = swap_cores(own_basis)
 
+    other_basis_down = swap_cores(after(basis_down, two_own))
     partial_up = project_up(place, own_basis, local_up, True)
     two[0] = after(two[0], partial_up)
     partial_up = project_up(place, other_basis, local_up, False, partial_up)
     partial_up = partial_up.reshape(4, 64, 512)
+
+    mine, theirs = (z, 3 - z), (z ^ 1, 3 - (z ^ 1))
+    half_up = jnp.stack([pick(partial_up, block) for block in theirs])
+    half_up = exchange(half_up, 1).astype(f32)
+    half_up = half_up + jnp.stack([pick(partial_up, block) for block in mine]).astype(f32)
 
     def part_three(k):
         index = (y + k) % 4
@@ -361,14 +392,15 @@
     proj_down = total(three[1:], three[0]) * (1.0 / replicas)
     new_moment_down, new_second_down, low_down = adam_update(proj_down, moment_down, second_down)
 
-    up = [pick(partial_up, z)] + [
-        shift(pick(partial_up, (z + k) % 4), "z", "z", k) for k in (2, 1, 3)
+    proj_up = (half_up[0] + exchange(half_up[1].astype(bf16), 3).astype(f32)) * (1.0 / replicas)
+    new_moment_up, new_second_up, low_up = adam_update(proj_up, moment_up, second_up)
+    pair_up = jnp.stack([low_up, exchange(low_up, 3)])
+    all_up = jnp.concatenate([pair_up, exchange(pair_up, 1)])
+    order = [
+        jnp.where(block == z, 0, jnp.where(block == 3 - z, 1, jnp.where(block == z ^ 1, 2, 3)))
+        for block in range(4)
     ]
-    proj_up = total(up[1:], up[0]) * (1.0 / replicas)
-    new_moment_up, new_second_up, low_up = adam_update(proj_up, moment_up, second_up)
-    gathered = jnp.stack([low_up] + [shift(low_up, "z", "z", k) for k in (1, 2, 3)])
-    gathered = jnp.stack([pick(gathered, (z + 4 - block) % 4) for block in range(4)])
-    all_low_up = gathered.reshape(256, 512)
+    all_low_up = jnp.stack([pick(all_up, at) for at in order]).reshape(256, 512)
 
     blocks = [
         lax.dynamic_index_in_dim(basis, (x + 4 - z) % 4, 1, keepdims=False)
@@ -387,6 +419,7 @@
         *blocks,
         all_low_up,
     )
+    sums = after(sums, *sibling)
     sums = lax.all_to_all(sums, AXES, 0, 0, tiled=True)
     new_weight_up, new_weight_down = update(
         place,

time: 147 us -> 132 us (0.90)
  waiting for transfers between devices: 40.4 us -> 20.8 us
  blocking collectives: 0 us -> 18.4 us
  starting transfers between devices: 57.4 us -> 48.1 us
  local copies, waits for them, and re-layouts: 11.4 us -> 7.53 us
  Pallas kernels: 26.3 us -> 24.4 us
    all_to_all x0 -> x1, blocking collectives: none -> 18.4 us  [per_device(): sums = lax.all_to_all(sums, AXES, 0, 0, tiled=True)]
    all_to_all x1 -> x0, waiting for transfers between devices: 9.32 us -> none  [per_device(): sums = lax.all_to_all(sums, AXES, 0, 0, tiled=True)]
    all_to_all x1 -> x0, starting transfers between devices: 7.62 us -> none  [per_device(): sums = lax.all_to_all(sums, AXES, 0, 0, tiled=True)]
    ppermute x8, waiting for transfers between devices: 6.71 us -> 0.31 us  [swap_cores(): return lax.ppermute(value, 'c', [(0, 1), (1, 0)])]
    ppermute x28 -> x22, starting transfers between devices: 36.1 us -> 31.1 us  [shift(): return lax.ppermute(value, AXES, shift_pairs(axis0, axis1, k))]
    unnamed x36 -> x26, local copies, waits for them, and re-layouts: 8.24 us -> 4.35 us
    ppermute x28 -> x22, waiting for transfers between devices: 24.3 us -> 20.4 us  [shift(): return lax.ppermute(value, AXES, shift_pairs(axis0, axis1, k))]
    ppermute x0 -> x4, starting transfers between devices: none -> 2.66 us  [exchange(): return lax.ppermute(value, 'z', [(i, i ^ mask) for i in range(4)])]
  transfers between devices with their start and end apart: 37 -> 34, of which waited for: 10 -> 11; matrix products, arithmetic and copies ran while one was open for 8% -> 10% of each run, Pallas kernels for 12% -> 12%
where the time goes in v2:
time: 132 us
  starting transfers between devices  48.1 us (36%)
  Pallas kernels  24.4 us (18%)
  waiting for transfers between devices  20.8 us (16%)
  blocking collectives  18.4 us (14%)
  other arithmetic  11.2 us (8%)
  local copies, waits for them, and re-layouts  7.53 us (6%)
    ppermute x22, starting transfers between devices, shift(): return lax.ppermute(value, AXES, shift_pairs(axis0, axis1, k))  31.1 us
    ppermute x22, waiting for transfers between devices, shift(): return lax.ppermute(value, AXES, shift_pairs(axis0, axis1, k))  20.4 us
    all_to_all x1, blocking collectives, per_device(): sums = lax.all_to_all(sums, AXES, 0, 0, tiled=True)  18.4 us
    ppermute x8, starting transfers between devices, swap_cores(): return lax.ppermute(value, 'c', [(0, 1), (1, 0)])  14.4 us
    pallas_call x2, Pallas kernels, project_up(): pl.pallas_call(project_up_kernel, out_shape=jax.ShapeDtypeStruct((256, 51...  10.3 us
    pallas_call x6, Pallas kernels, project_rows(): pl.pallas_call(functools.partial(project_kernel, other is not None), out_...  7.32 us
    unnamed x26, local copies, waits for them, and re-layouts  4.35 us
    pallas_call x1, Pallas kernels, update(): pl.pallas_call(update_kernel, out_shape=[jax.ShapeDtypeStruct(weight_up.s...  3.83 us
  transfers between devices with their start and end apart: 34, of which 11 were waited for; matrix products, arithmetic and copies ran while one was open for 10% of the time, Pallas kernels for 12%

profile of v2, /device:TPU:1, one launch (start us, length us, event | category | flops | bytes accessed | tf_op | source)
XLA Modules:
  0.0 131.7 jit_solution(7189154693457754677)
XLA Ops:
  0.7 3.4 %copy-done = bf16[1,16384,256]{2,1,0:T(8,128)(2,1)S(1)} copy-done((bf16[1,16384,256]{2,1,0:T(8,128)(2,1)S(1)}, bf16[1,16384,256]{2,1,0:T(8,128)(2,1)}, u32[]{:S(2)}) %copy-start) | copy-done | bytes 8388632
  6.0 1.5 %collective-permute-start = (bf16[1,4,4,128,256]{4,3,2,1,0:T(8,128)(2,1)S(1)}, bf16[1,4,4,128,256]{4,3,2,1,0:T(8,128)(2,1)S(1)}, u32[]{:S(2)}, u32[]{:S(2)}) collective-permute-start(bf16[1,4,4,128,256]{4,3,2,1,0:T(8,128)(2,1)S(1)} %shard_map.145), channel_id=1, source_target_pairs={{0,1},{1,0},{2,3},{3,2},{4,5},{5,4},{6,7},{7,6},{8,9},{9,8},{10,11... | collective-permute-start | bytes 3145736 | tf_op jit(solution)/shard_map/ppermute | solution.py:52
  7.5 2.8 %collective-permute-start.2 = (bf16[256,256]{1,0:T(8,128)(2,1)S(1)}, bf16[256,256]{1,0:T(8,128)(2,1)S(1)}, u32[]{:S(2)}, u32[]{:S(2)}) collective-permute-start(bf16[256,256]{1,0:T(8,128)(2,1)S(1)} %copy-done.12), channel_id=1, source_target_pairs={{0,16},{1,17},{2,18},{3,19},{4,20},{5,21},{6,22},{7,23},{8,24},{9,... | collective-permute-start | bytes 393224 | tf_op jit(solution)/shard_map/ppermute | solution.py:48
  11.8 2.3 %collective-permute-done.2 = bf16[256,256]{1,0:T(8,128)(2,1)S(1)} collective-permute-done((bf16[256,256]{1,0:T(8,128)(2,1)S(1)}, bf16[256,256]{1,0:T(8,128)(2,1)S(1)}, u32[]{:S(2)}, u32[]{:S(2)}) %collective-permute-start.2) | collective-permute-done | bytes 131104 | tf_op jit(solution)/shard_map/ppermute | solution.py:48
  14.1 3.0 %collective-permute-done.3 = bf16[256,256]{1,0:T(8,128)(2,1)S(1)} collective-permute-done((bf16[256,256]{1,0:T(8,128)(2,1)S(1)}, bf16[256,256]{1,0:T(8,128)(2,1)S(1)}, u32[]{:S(2)}, u32[]{:S(2)}) %collective-permute-start.3) | collective-permute-done | bytes 131104 | tf_op jit(solution)/shard_map/ppermute | solution.py:48
  18.1 2.4 %shard_map.147 = bf16[3,4,4,128,256]{4,3,2,1,0:T(8,128)(2,1)S(1)} custom-call(s32[4]{0:T(128)S(1)} %pad_add_fusion.place_ref, bf16[4,4,4,2,128,256]{5,4,3,2,1,0:T(8,128)(2,1)S(1)} %bitcast.68, bf16[4,4,4,2,128,256]{5,4,3,2,1,0:T(8,128)(2,1)S(1)} %bitcast.66, bf16[4,4,4,2,128,256]{5,4,3,2,1,0:T(8,128)(2,1)S(1)} %bitcast.67, ...), custom_call_target="tpu_custom_call" | custom-call | flops 3 | bytes 3 | tf_op jit(solution)/shard_map/pallas_call | solution.py:104
  21.9 2.7 %collective-permute-start.10 = (bf16[4,256,256]{2,1,0:T(8,128)(2,1)S(1)}, bf16[4,256,256]{2,1,0:T(8,128)(2,1)S(1)}, u32[]{:S(2)}, u32[]{:S(2)}) collective-permute-start(bf16[4,256,256]{2,1,0:T(8,128)(2,1)S(1)} %pad_maximum_fusion.1), channel_id=1, source_target_pairs={{0,6},{1,7},{2,0},{3,1},{4,2},{5,3},{6,4},{7,5},{8,14},{9,15},{10,... | collective-permute-start | bytes 1572872 | tf_op jit(solution)/shard_map/ppermute | solution.py:48
  24.7 2.2 %collective-permute-start.5 = (bf16[4,4,128,256]{3,2,1,0:T(8,128)(2,1)S(1)}, bf16[4,4,128,256]{3,2,1,0:T(8,128)(2,1)S(1)}, u32[]{:S(2)}, u32[]{:S(2)}) collective-permute-start(bf16[4,4,128,256]{3,2,1,0:T(8,128)(2,1)S(1)} %bitcast.84), channel_id=1, source_target_pairs={{0,64},{1,17},{2,66},{3,19},{4,68},{5,21},{6,70},{7,23},{8,72},{9,... | collective-permute-start | bytes 3145736 | tf_op jit(solution)/shard_map/ppermute | solution.py:48
  29.2 2.0 %collective-permute-start.7 = (bf16[4,4,128,256]{3,2,1,0:T(8,128)(2,1)S(1)}, bf16[4,4,128,256]{3,2,1,0:T(8,128)(2,1)S(1)}, u32[]{:S(2)}, u32[]{:S(2)}) collective-permute-start(bf16[4,4,128,256]{3,2,1,0:T(8,128)(2,1)S(1)} %bitcast.86), channel_id=1, source_target_pairs={{0,96},{1,25},{2,98},{3,27},{4,100},{5,29},{6,102},{7,31},{8,104},... | collective-permute-start | bytes 3145736 | tf_op jit(solution)/shard_map/ppermute | solution.py:48
  31.2 4.7 %collective-permute-done.10 = bf16[4,256,256]{2,1,0:T(8,128)(2,1)S(1)} collective-permute-done((bf16[4,256,256]{2,1,0:T(8,128)(2,1)S(1)}, bf16[4,256,256]{2,1,0:T(8,128)(2,1)S(1)}, u32[]{:S(2)}, u32[]{:S(2)}) %collective-permute-start.10) | collective-permute-done | bytes 524320 | tf_op jit(solution)/shard_map/ppermute | solution.py:48
  36.0 3.1 %collective-permute-done.8 = bf16[4,256,256]{2,1,0:T(8,128)(2,1)S(1)} collective-permute-done((bf16[4,256,256]{2,1,0:T(8,128)(2,1)S(1)}, bf16[4,256,256]{2,1,0:T(8,128)(2,1)S(1)}, u32[]{:S(2)}, u32[]{:S(2)}) %collective-permute-start.8) | collective-permute-done | bytes 524320 | tf_op jit(solution)/shard_map/ppermute | solution.py:48
  41.6 1.7 %multiply_reduce_fusion = f32[]{:T(128)} fusion(bf16[4096,256]{1,0:T(8,128)(2,1)S(1)} %copy-done.1), kind=kLoop, calls=%fused_computation | loop fusion | flops 3145727 | bytes 2097156 | tf_op jit(solution)/shard_map/reduce_sum | solution.py:348
  43.3 1.7 %multiply_reduce_fusion.1 = f32[]{:T(128)} fusion(bf16[2048,512]{1,0:T(8,128)(2,1)S(1)} %copy-done.2), kind=kLoop, calls=%fused_computation.1 | loop fusion | flops 3145727 | bytes 2097156 | tf_op jit(solution)/shard_map/reduce_sum | solution.py:347
  45.0 1.7 %collective-permute-done.11 = bf16[2,256,256]{2,1,0:T(8,128)(2,1)S(1)} collective-permute-done((bf16[2,256,256]{2,1,0:T(8,128)(2,1)S(1)}, bf16[2,256,256]{2,1,0:T(8,128)(2,1)S(1)}, u32[]{:S(2)}, u32[]{:S(2)}) %collective-permute-start.11) | collective-permute-done | bytes 262176 | tf_op jit(solution)/shard_map/ppermute | solution.py:48
  46.8 1.6 %collective-permute-done.9 = bf16[2,256,256]{2,1,0:T(8,128)(2,1)S(1)} collective-permute-done((bf16[2,256,256]{2,1,0:T(8,128)(2,1)S(1)}, bf16[2,256,256]{2,1,0:T(8,128)(2,1)S(1)}, u32[]{:S(2)}, u32[]{:S(2)}) %collective-permute-start.9) | collective-permute-done | bytes 262176 | tf_op jit(solution)/shard_map/ppermute | solution.py:48
  48.4 2.6 %collective-permute-done.7.refs_2_ = bf16[4,4,128,256]{3,2,1,0:T(8,128)(2,1)S(1)} collective-permute-done((bf16[4,4,128,256]{3,2,1,0:T(8,128)(2,1)S(1)}, bf16[4,4,128,256]{3,2,1,0:T(8,128)(2,1)S(1)}, u32[]{:S(2)}, u32[]{:S(2)}) %collective-permute-start.7) | collective-permute-done | bytes 1048608 | tf_op jit(solution)/shard_map/ppermute | solution.py:48
  52.4 1.6 %pad_maximum_fusion.basis_ref = bf16[4,4,256,256]{3,2,1,0:T(8,128)(2,1)} fusion(bf16[1,4,256,256]{3,2,1,0:T(8,128)(2,1)S(1)} %bitcast.106, bf16[1,4,256,256]{3,2,1,0:T(8,128)(2,1)S(1)} %maximum_bitcast_fusion, bf16[1,4,256,256]{3,2,1,0:T(8,128)(2,1)S(1)} %bitcast.107, bf16[1,4,256,256]{3,2,1,0:T(8,128)(2,1)S(1)} %bitcast.105), kind=kLoop, calls=%fused_computation.2 | loop fusion | flops 3145728 | bytes 4194304 | tf_op jit(solution)/shard_map/stack | solution.py:370
  54.0 2.6 %collective-permute-start.15 = (bf16[4,4,256,256]{3,2,1,0:T(8,128)(2,1)}, bf16[4,4,256,256]{3,2,1,0:T(8,128)(2,1)}, u32[]{:S(2)}, u32[]{:S(2)}) collective-permute-start(bf16[4,4,256,256]{3,2,1,0:T(8,128)(2,1)} %pad_maximum_fusion.basis_ref), channel_id=1, source_target_pairs={{0,1},{1,0},{2,3},{3,2},{4,5},{5,4},{6,7},{7,6},{8,9},{9,8},{10,11... | collective-permute-start | bytes 6291464 | tf_op jit(solution)/shard_map/ppermute | solution.py:52
  56.6 5.1 %shard_map.152.refs_8_ = f32[256,512]{1,0:T(8,128)} custom-call(s32[4]{0:T(128)} %copy-done.6, bf16[4,4,256,256]{3,2,1,0:T(8,128)(2,1)} %pad_maximum_fusion.basis_ref, bf16[8192,512]{1,0:T(8,128)(2,1)} %bitcast.89, bf16[8192,512]{1,0:T(8,128)(2,1)} %bitcast.90, bf16[8192,512]{1,0:T(8,128)(2,1)} %bitcast.91, bf16[8192,512]{1,0:T(8,128)(2,1)} %bitcast.92, ...), custom_call_target="tpu_custom_call" | custom-call | flops 1 | bytes 1 | tf_op jit(solution)/shard_map/pallas_call | solution.py:160
  61.7 2.2 %collective-permute-start.12 = (bf16[4,128,256]{2,1,0:T(8,128)(2,1)S(1)}, bf16[4,128,256]{2,1,0:T(8,128)(2,1)}, u32[]{:S(2)}, u32[]{:S(2)}) collective-permute-start(bf16[4,128,256]{2,1,0:T(8,128)(2,1)S(1)} %get-tuple-element.32), channel_id=1, source_target_pairs={{0,16},{1,65},{2,18},{3,67},{4,20},{5,69},{6,22},{7,71},{8,24},{9,... | collective-permute-start | bytes 786440 | tf_op jit(solution)/shard_map/ppermute | solution.py:48
  64.7 1.9 %collective-permute-start.14 = (bf16[4,128,256]{2,1,0:T(8,128)(2,1)S(1)}, bf16[4,128,256]{2,1,0:T(8,128)(2,1)}, u32[]{:S(2)}, u32[]{:S(2)}) collective-permute-start(bf16[4,128,256]{2,1,0:T(8,128)(2,1)S(1)} %get-tuple-element.34), channel_id=1, source_target_pairs={{0,24},{1,97},{2,26},{3,99},{4,28},{5,101},{6,30},{7,103},{8,0},{9... | collective-permute-start | bytes 786440 | tf_op jit(solution)/shard_map/ppermute | solution.py:48
  66.6 5.2 %shard_map.153 = bf16[256,512]{1,0:T(8,128)(2,1)} custom-call(s32[4]{0:T(128)} %copy-done.6, bf16[4,4,256,256]{3,2,1,0:T(8,128)(2,1)} %collective-permute-done.15.basis_ref, bf16[8192,512]{1,0:T(8,128)(2,1)} %bitcast.97, bf16[8192,512]{1,0:T(8,128)(2,1)} %bitcast.98, bf16[8192,512]{1,0:T(8,128)(2,1)} %bitcast.99, bf16[8192,512]{1,0:T(8,128)(2,1)} %bitcast.100, ...), custom_call_target="tpu_custom_call" | custom-call | flops 1 | bytes 1 | tf_op jit(solution)/shard_map/pallas_call | solution.py:160
  76.3 2.0 %collective-permute-start.16 = (bf16[128,256]{1,0:T(8,128)(2,1)S(1)}, bf16[128,256]{1,0:T(8,128)(2,1)S(1)}, u32[]{:S(2)}, u32[]{:S(2)}) collective-permute-start(bf16[128,256]{1,0:T(8,128)(2,1)S(1)} %get-tuple-element.46), channel_id=1, source_target_pairs={{0,4},{1,5},{2,6},{3,7},{4,0},{5,1},{6,2},{7,3},{8,12},{9,13},{10,... | collective-permute-start | bytes 196616 | tf_op jit(solution)/shard_map/ppermute | solution.py:48
  78.3 1.6 %collective-permute-start.17 = (bf16[128,256]{1,0:T(8,128)(2,1)S(1)}, bf16[128,256]{1,0:T(8,128)(2,1)S(1)}, u32[]{:S(2)}, u32[]{:S(2)}) collective-permute-start(bf16[128,256]{1,0:T(8,128)(2,1)S(1)} %get-tuple-element.48), channel_id=1, source_target_pairs={{0,2},{1,3},{2,4},{3,5},{4,6},{5,7},{6,0},{7,1},{8,10},{9,11},{10,... | collective-permute-start | bytes 196616 | tf_op jit(solution)/shard_map/ppermute | solution.py:48
  84.9 2.5 %collective-permute-start.20 = (bf16[128,256]{1,0:T(8,128)(2,1)S(1)}, bf16[128,256]{1,0:T(8,128)(2,1)S(1)}, u32[]{:S(2)}, u32[]{:S(2)}) collective-permute-start(bf16[128,256]{1,0:T(8,128)(2,1)S(1)} %get-tuple-element.43), channel_id=1, source_target_pairs={{0,4},{1,17},{2,6},{3,19},{4,0},{5,21},{6,2},{7,23},{8,12},{9,25},... | collective-permute-start | bytes 196616 | tf_op jit(solution)/shard_map/ppermute | solution.py:48
  87.4 1.6 %collective-permute-start.21 = (bf16[128,256]{1,0:T(8,128)(2,1)S(1)}, bf16[128,256]{1,0:T(8,128)(2,1)S(1)}, u32[]{:S(2)}, u32[]{:S(2)}) collective-permute-start(bf16[128,256]{1,0:T(8,128)(2,1)S(1)} %get-tuple-element.43), channel_id=1, source_target_pairs={{0,6},{1,25},{2,0},{3,27},{4,2},{5,29},{6,4},{7,31},{8,14},{9,1},{... | collective-permute-start | bytes 196616 | tf_op jit(solution)/shard_map/ppermute | solution.py:48
  91.2 3.3 %collective-permute-start.23 = (bf16[4,128,256]{2,1,0:T(8,128)(2,1)S(1)}, bf16[4,128,256]{2,1,0:T(8,128)(2,1)S(1)}, u32[]{:S(2)}, u32[]{:S(2)}) collective-permute-start(bf16[4,128,256]{2,1,0:T(8,128)(2,1)S(1)} %pad_maximum_fusion.2.refs_0_), channel_id=1, source_target_pairs={{0,16},{1,5},{2,18},{3,7},{4,20},{5,1},{6,22},{7,3},{8,24},{9,13},... | collective-permute-start | bytes 786440 | tf_op jit(solution)/shard_map/ppermute | solution.py:48
  97.2 4.2 %collective-permute-start.25 = (bf16[256,256]{1,0:T(8,128)(2,1)S(1)}, bf16[256,256]{1,0:T(8,128)(2,1)S(1)}, u32[]{:S(2)}, u32[]{:S(2)}) collective-permute-start(bf16[256,256]{1,0:T(8,128)(2,1)S(1)} %copy-done.5), channel_id=1, source_target_pairs={{0,1},{1,0},{2,3},{3,2},{4,5},{5,4},{6,7},{7,6},{8,9},{9,8},{10,11... | collective-permute-start | bytes 393224 | tf_op jit(solution)/shard_map/ppermute | solution.py:52
  102.5 3.8 %collective-permute-start.30 = (bf16[4,128,256]{2,1,0:T(8,128)(2,1)S(1)}, bf16[4,128,256]{2,1,0:T(8,128)(2,1)S(1)}, u32[]{:S(2)}, u32[]{:S(2)}) collective-permute-start(bf16[4,128,256]{2,1,0:T(8,128)(2,1)S(1)} %pad_maximum_fusion.2.refs_0_), channel_id=1, source_target_pairs={{0,1},{1,0},{2,3},{3,2},{4,5},{5,4},{6,7},{7,6},{8,9},{9,8},{10,11... | collective-permute-start | bytes 786440 | tf_op jit(solution)/shard_map/ppermute | solution.py:52
  107.4 1.9 %shard_map.154 = f32[128,1,128]{2,1,0:T(1,128)S(1)} custom-call(f32[2]{0:T(128)S(1)} %pad_maximum_fusion.7.weights_ref, bf16[4,128,256]{2,1,0:T(8,128)(2,1)S(1)} %pad_maximum_fusion.2.refs_0_, bf16[4,128,256]{2,1,0:T(8,128)(2,1)S(1)} %collective-permute-done.22.refs_1_, bf16[4,128,256]{2,1,0:T(8,128)(2,1)S(1)} %collective-permute-done.23.refs_2_, ...), custom_call_target="tpu_custom_call" | custom-call | flops 17179869184 | bytes 3145728 | tf_op jit(solution)/shard_map/pallas_call | solution.py:232
  109.3 18.4 %all_to_all.5.sums_ref = f32[128,1,128]{2,1,0:T(1,128)S(1)} all-to-all(f32[128,1,128]{2,1,0:T(1,128)S(1)} %shard_map.154), channel_id=1, replica_groups=mesh['z'=4,'x'=4,'y'=4,'c'=2] {'z','x','y','c'}, dimensions={0} | all-to-all | bytes 131072 | tf_op jit(solution)/shard_map/all_to_all | solution.py:423
  127.7 3.8 %shard_map.155 = (bf16[4,2,256,512]{3,2,1,0:T(8,128)(2,1)}, bf16[4,4,2,128,256]{4,3,2,1,0:T(8,128)(2,1)}) custom-call(s32[4]{0:T(128)S(1)} %copy-done.7, f32[128,1,128]{2,1,0:T(1,128)S(1)} %all_to_all.5.sums_ref, bf16[4,128,256]{2,1,0:T(8,128)(2,1)S(1)} %pad_maximum_fusion.2.refs_0_, bf16[4,128,256]{2,1,0:T(8,128)(2,1)S(1)} %collective-permute-done.22.refs_1_, ...), custom_call_target="tpu_custom_call" | custom-call | flops 1073741824 | bytes 11534336 | tf_op jit(solution)/shard_map/pallas_call | solution.py:294
  (97 shorter events, 29.3 us)
Async XLA Ops:
  6.0 11.1 %collective-permute-start = (bf16[1,4,4,128,256]{4,3,2,1,0:T(8,128)(2,1)S(1)}, bf16[1,4,4,128,256]{4,3,2,1,0:T(8,128)(2,1)S(1)}, u32[]{:S(2)}, u32[]{:S(2)}) collective-permute-start(bf16[1,4,4,128,256]{4,3,2,1,0:T(8,128)(2,1)S(1)} %shard_map.145), channel_id=1, source_target_pairs={{0,1},{1,0},{2,3},{3,2},{4,5},{5,4},{6,7},{7,6},{8,9},{9,8},{10,11... | collective-permute-start | bytes 3145736 | tf_op jit(solution)/shard_map/ppermute | solution.py:52
  7.5 6.6 %collective-permute-start.2 = (bf16[256,256]{1,0:T(8,128)(2,1)S(1)}, bf16[256,256]{1,0:T(8,128)(2,1)S(1)}, u32[]{:S(2)}, u32[]{:S(2)}) collective-permute-start(bf16[256,256]{1,0:T(8,128)(2,1)S(1)} %copy-done.12), channel_id=1, source_target_pairs={{0,16},{1,17},{2,18},{3,19},{4,20},{5,21},{6,22},{7,23},{8,24},{9,... | collective-permute-start | bytes 393224 | tf_op jit(solution)/shard_map/ppermute | solution.py:48
  10.3 6.7 %collective-permute-start.3 = (bf16[256,256]{1,0:T(8,128)(2,1)S(1)}, bf16[256,256]{1,0:T(8,128)(2,1)S(1)}, u32[]{:S(2)}, u32[]{:S(2)}) collective-permute-start(bf16[256,256]{1,0:T(8,128)(2,1)S(1)} %copy-done.12), channel_id=1, source_target_pairs={{0,24},{1,25},{2,26},{3,27},{4,28},{5,29},{6,30},{7,31},{8,0},{9,1... | collective-permute-start | bytes 393224 | tf_op jit(solution)/shard_map/ppermute | solution.py:48
  11.2 5.8 %collective-permute-start.1 = (bf16[256,256]{1,0:T(8,128)(2,1)S(1)}, bf16[256,256]{1,0:T(8,128)(2,1)S(1)}, u32[]{:S(2)}, u32[]{:S(2)}) collective-permute-start(bf16[256,256]{1,0:T(8,128)(2,1)S(1)} %copy-done.12), channel_id=1, source_target_pairs={{0,8},{1,9},{2,10},{3,11},{4,12},{5,13},{6,14},{7,15},{8,16},{9,17... | collective-permute-start | bytes 393224 | tf_op jit(solution)/shard_map/ppermute | solution.py:48
  20.5 6.7 %collective-permute-start.4 = (bf16[3,4,4,128,256]{4,3,2,1,0:T(8,128)(2,1)S(1)}, bf16[3,4,4,128,256]{4,3,2,1,0:T(8,128)(2,1)S(1)}, u32[]{:S(2)}, u32[]{:S(2)}) collective-permute-start(bf16[3,4,4,128,256]{4,3,2,1,0:T(8,128)(2,1)S(1)} %shard_map.147), channel_id=1, source_target_pairs={{0,1},{1,0},{2,3},{3,2},{4,5},{5,4},{6,7},{7,6},{8,9},{9,8},{10,11... | collective-permute-start | bytes 9437192 | tf_op jit(solution)/shard_map/ppermute | solution.py:52
  21.9 14.0 %collective-permute-start.10 = (bf16[4,256,256]{2,1,0:T(8,128)(2,1)S(1)}, bf16[4,256,256]{2,1,0:T(8,128)(2,1)S(1)}, u32[]{:S(2)}, u32[]{:S(2)}) collective-permute-start(bf16[4,256,256]{2,1,0:T(8,128)(2,1)S(1)} %pad_maximum_fusion.1), channel_id=1, source_target_pairs={{0,6},{1,7},{2,0},{3,1},{4,2},{5,3},{6,4},{7,5},{8,14},{9,15},{10,... | collective-permute-start | bytes 1572872 | tf_op jit(solution)/shard_map/ppermute | solution.py:48
  24.7 14.4 %collective-permute-start.8 = (bf16[4,256,256]{2,1,0:T(8,128)(2,1)S(1)}, bf16[4,256,256]{2,1,0:T(8,128)(2,1)S(1)}, u32[]{:S(2)}, u32[]{:S(2)}) collective-permute-start(bf16[4,256,256]{2,1,0:T(8,128)(2,1)S(1)} %pad_maximum_fusion.1), channel_id=1, source_target_pairs={{0,2},{1,3},{2,4},{3,5},{4,6},{5,7},{6,0},{7,1},{8,10},{9,11},{10,... | collective-permute-start | bytes 1572872 | tf_op jit(solution)/shard_map/ppermute | solution.py:48
  24.7 23.7 %collective-permute-start.5 = (bf16[4,4,128,256]{3,2,1,0:T(8,128)(2,1)S(1)}, bf16[4,4,128,256]{3,2,1,0:T(8,128)(2,1)S(1)}, u32[]{:S(2)}, u32[]{:S(2)}) collective-permute-start(bf16[4,4,128,256]{3,2,1,0:T(8,128)(2,1)S(1)} %bitcast.84), channel_id=1, source_target_pairs={{0,64},{1,17},{2,66},{3,19},{4,68},{5,21},{6,70},{7,23},{8,72},{9,... | collective-permute-start | bytes 3145736 | tf_op jit(solution)/shard_map/ppermute | solution.py:48
  29.2 21.8 %collective-permute-start.7 = (bf16[4,4,128,256]{3,2,1,0:T(8,128)(2,1)S(1)}, bf16[4,4,128,256]{3,2,1,0:T(8,128)(2,1)S(1)}, u32[]{:S(2)}, u32[]{:S(2)}) collective-permute-start(bf16[4,4,128,256]{3,2,1,0:T(8,128)(2,1)S(1)} %bitcast.86), channel_id=1, source_target_pairs={{0,96},{1,25},{2,98},{3,27},{4,100},{5,29},{6,102},{7,31},{8,104},... | collective-permute-start | bytes 3145736 | tf_op jit(solution)/shard_map/ppermute | solution.py:48
  31.2 20.1 %collective-permute-start.6 = (bf16[4,4,128,256]{3,2,1,0:T(8,128)(2,1)S(1)}, bf16[4,4,128,256]{3,2,1,0:T(8,128)(2,1)S(1)}, u32[]{:S(2)}, u32[]{:S(2)}) collective-permute-start(bf16[4,4,128,256]{3,2,1,0:T(8,128)(2,1)S(1)} %bitcast.85), channel_id=1, source_target_pairs={{0,32},{1,9},{2,34},{3,11},{4,36},{5,13},{6,38},{7,15},{8,40},{9,1... | collective-permute-start | bytes 3145736 | tf_op jit(solution)/shard_map/ppermute | solution.py:48
  40.1 6.7 %collective-permute-start.11 = (bf16[2,256,256]{2,1,0:T(8,128)(2,1)S(1)}, bf16[2,256,256]{2,1,0:T(8,128)(2,1)S(1)}, u32[]{:S(2)}, u32[]{:S(2)}) collective-permute-start(bf16[2,256,256]{2,1,0:T(8,128)(2,1)S(1)} %slice.18), channel_id=1, source_target_pairs={{0,6},{1,7},{2,0},{3,1},{4,2},{5,3},{6,4},{7,5},{8,14},{9,15},{10,... | collective-permute-start | bytes 786440 | tf_op jit(solution)/shard_map/ppermute | solution.py:48
  40.5 7.9 %collective-permute-start.9 = (bf16[2,256,256]{2,1,0:T(8,128)(2,1)S(1)}, bf16[2,256,256]{2,1,0:T(8,128)(2,1)S(1)}, u32[]{:S(2)}, u32[]{:S(2)}) collective-permute-start(bf16[2,256,256]{2,1,0:T(8,128)(2,1)S(1)} %slice.17), channel_id=1, source_target_pairs={{0,2},{1,3},{2,4},{3,5},{4,6},{5,7},{6,0},{7,1},{8,10},{9,11},{10,... | collective-permute-start | bytes 786440 | tf_op jit(solution)/shard_map/ppermute | solution.py:48
  54.0 12.6 %collective-permute-start.15 = (bf16[4,4,256,256]{3,2,1,0:T(8,128)(2,1)}, bf16[4,4,256,256]{3,2,1,0:T(8,128)(2,1)}, u32[]{:S(2)}, u32[]{:S(2)}) collective-permute-start(bf16[4,4,256,256]{3,2,1,0:T(8,128)(2,1)} %pad_maximum_fusion.basis_ref), channel_id=1, source_target_pairs={{0,1},{1,0},{2,3},{3,2},{4,5},{5,4},{6,7},{7,6},{8,9},{9,8},{10,11... | collective-permute-start | bytes 6291464 | tf_op jit(solution)/shard_map/ppermute | solution.py:52
  61.7 13.1 %collective-permute-start.12 = (bf16[4,128,256]{2,1,0:T(8,128)(2,1)S(1)}, bf16[4,128,256]{2,1,0:T(8,128)(2,1)}, u32[]{:S(2)}, u32[]{:S(2)}) collective-permute-start(bf16[4,128,256]{2,1,0:T(8,128)(2,1)S(1)} %get-tuple-element.32), channel_id=1, source_target_pairs={{0,16},{1,65},{2,18},{3,67},{4,20},{5,69},{6,22},{7,71},{8,24},{9,... | collective-permute-start | bytes 786440 | tf_op jit(solution)/shard_map/ppermute | solution.py:48
  63.9 10.9 %collective-permute-start.13 = (bf16[4,128,256]{2,1,0:T(8,128)(2,1)S(1)}, bf16[4,128,256]{2,1,0:T(8,128)(2,1)}, u32[]{:S(2)}, u32[]{:S(2)}) collective-permute-start(bf16[4,128,256]{2,1,0:T(8,128)(2,1)S(1)} %get-tuple-element.33), channel_id=1, source_target_pairs={{0,8},{1,33},{2,10},{3,35},{4,12},{5,37},{6,14},{7,39},{8,16},{9,4... | collective-permute-start | bytes 786440 | tf_op jit(solution)/shard_map/ppermute | solution.py:48
  64.7 10.2 %collective-permute-start.14 = (bf16[4,128,256]{2,1,0:T(8,128)(2,1)S(1)}, bf16[4,128,256]{2,1,0:T(8,128)(2,1)}, u32[]{:S(2)}, u32[]{:S(2)}) collective-permute-start(bf16[4,128,256]{2,1,0:T(8,128)(2,1)S(1)} %get-tuple-element.34), channel_id=1, source_target_pairs={{0,24},{1,97},{2,26},{3,99},{4,28},{5,101},{6,30},{7,103},{8,0},{9... | collective-permute-start | bytes 786440 | tf_op jit(solution)/shard_map/ppermute | solution.py:48
  73.4 7.5 %collective-permute-start.26 = (bf16[2,64,512]{2,1,0:T(8,128)(2,1)}, bf16[2,64,512]{2,1,0:T(8,128)(2,1)}, u32[]{:S(2)}, u32[]{:S(2)}) collective-permute-start(bf16[2,64,512]{2,1,0:T(8,128)(2,1)} %pad_maximum_fusion.5), channel_id=1, source_target_pairs={{0,32},{32,0},{64,96},{96,64},{1,33},{33,1},{65,97},{97,65},{2,34}... | collective-permute-start | bytes 393224 | tf_op jit(solution)/shard_map/ppermute | solution.py:56
  76.3 5.9 %collective-permute-start.16 = (bf16[128,256]{1,0:T(8,128)(2,1)S(1)}, bf16[128,256]{1,0:T(8,128)(2,1)S(1)}, u32[]{:S(2)}, u32[]{:S(2)}) collective-permute-start(bf16[128,256]{1,0:T(8,128)(2,1)S(1)} %get-tuple-element.46), channel_id=1, source_target_pairs={{0,4},{1,5},{2,6},{3,7},{4,0},{5,1},{6,2},{7,3},{8,12},{9,13},{10,... | collective-permute-start | bytes 196616 | tf_op jit(solution)/shard_map/ppermute | solution.py:48
  78.3 4.3 %collective-permute-start.17 = (bf16[128,256]{1,0:T(8,128)(2,1)S(1)}, bf16[128,256]{1,0:T(8,128)(2,1)S(1)}, u32[]{:S(2)}, u32[]{:S(2)}) collective-permute-start(bf16[128,256]{1,0:T(8,128)(2,1)S(1)} %get-tuple-element.48), channel_id=1, source_target_pairs={{0,2},{1,3},{2,4},{3,5},{4,6},{5,7},{6,0},{7,1},{8,10},{9,11},{10,... | collective-permute-start | bytes 196616 | tf_op jit(solution)/shard_map/ppermute | solution.py:48
  79.9 3.4 %collective-permute-start.18 = (bf16[128,256]{1,0:T(8,128)(2,1)S(1)}, bf16[128,256]{1,0:T(8,128)(2,1)S(1)}, u32[]{:S(2)}, u32[]{:S(2)}) collective-permute-start(bf16[128,256]{1,0:T(8,128)(2,1)S(1)} %get-tuple-element.47), channel_id=1, source_target_pairs={{0,6},{1,7},{2,0},{3,1},{4,2},{5,3},{6,4},{7,5},{8,14},{9,15},{10,... | collective-permute-start | bytes 196616 | tf_op jit(solution)/shard_map/ppermute | solution.py:48
  82.0 7.0 %collective-permute-start.27 = (bf16[64,512]{1,0:T(8,128)(2,1)S(1)}, bf16[64,512]{1,0:T(8,128)(2,1)S(1)}, u32[]{:S(2)}, u32[]{:S(2)}) collective-permute-start(bf16[64,512]{1,0:T(8,128)(2,1)S(1)} %fusion.4), channel_id=1, source_target_pairs={{0,96},{32,64},{64,32},{96,0},{1,97},{33,65},{65,33},{97,1},{2,98}... | collective-permute-start | bytes 196616 | tf_op jit(solution)/shard_map/ppermute | solution.py:56
  84.1 6.6 %collective-permute-start.19 = (bf16[128,256]{1,0:T(8,128)(2,1)S(1)}, bf16[128,256]{1,0:T(8,128)(2,1)S(1)}, u32[]{:S(2)}, u32[]{:S(2)}) collective-permute-start(bf16[128,256]{1,0:T(8,128)(2,1)S(1)} %get-tuple-element.43), channel_id=1, source_target_pairs={{0,2},{1,9},{2,4},{3,11},{4,6},{5,13},{6,0},{7,15},{8,10},{9,17},{... | collective-permute-start | bytes 196616 | tf_op jit(solution)/shard_map/ppermute | solution.py:48
  84.9 5.8 %collective-permute-start.20 = (bf16[128,256]{1,0:T(8,128)(2,1)S(1)}, bf16[128,256]{1,0:T(8,128)(2,1)S(1)}, u32[]{:S(2)}, u32[]{:S(2)}) collective-permute-start(bf16[128,256]{1,0:T(8,128)(2,1)S(1)} %get-tuple-element.43), channel_id=1, source_target_pairs={{0,4},{1,17},{2,6},{3,19},{4,0},{5,21},{6,2},{7,23},{8,12},{9,25},... | collective-permute-start | bytes 196616 | tf_op jit(solution)/shard_map/ppermute | solution.py:48
  87.4 3.3 %collective-permute-start.21 = (bf16[128,256]{1,0:T(8,128)(2,1)S(1)}, bf16[128,256]{1,0:T(8,128)(2,1)S(1)}, u32[]{:S(2)}, u32[]{:S(2)}) collective-permute-start(bf16[128,256]{1,0:T(8,128)(2,1)S(1)} %get-tuple-element.43), channel_id=1, source_target_pairs={{0,6},{1,25},{2,0},{3,27},{4,2},{5,29},{6,4},{7,31},{8,14},{9,1},{... | collective-permute-start | bytes 196616 | tf_op jit(solution)/shard_map/ppermute | solution.py:48
  89.7 4.9 %collective-permute-start.28 = (bf16[64,512]{1,0:T(8,128)(2,1)S(1)}, bf16[64,512]{1,0:T(8,128)(2,1)S(1)}, u32[]{:S(2)}, u32[]{:S(2)}) collective-permute-start(bf16[64,512]{1,0:T(8,128)(2,1)S(1)} %get-tuple-element.40), channel_id=1, source_target_pairs={{0,96},{32,64},{64,32},{96,0},{1,97},{33,65},{65,33},{97,1},{2,98}... | collective-permute-start | bytes 196616 | tf_op jit(solution)/shard_map/ppermute | solution.py:56
  90.7 11.7 %collective-permute-start.22 = (bf16[4,128,256]{2,1,0:T(8,128)(2,1)S(1)}, bf16[4,128,256]{2,1,0:T(8,128)(2,1)S(1)}, u32[]{:S(2)}, u32[]{:S(2)}) collective-permute-start(bf16[4,128,256]{2,1,0:T(8,128)(2,1)S(1)} %pad_maximum_fusion.2.refs_0_), channel_id=1, source_target_pairs={{0,8},{1,3},{2,10},{3,5},{4,12},{5,7},{6,14},{7,1},{8,16},{9,11},{... | collective-permute-start | bytes 786440 | tf_op jit(solution)/shard_map/ppermute | solution.py:48
  91.2 15.1 %collective-permute-start.23 = (bf16[4,128,256]{2,1,0:T(8,128)(2,1)S(1)}, bf16[4,128,256]{2,1,0:T(8,128)(2,1)S(1)}, u32[]{:S(2)}, u32[]{:S(2)}) collective-permute-start(bf16[4,128,256]{2,1,0:T(8,128)(2,1)S(1)} %pad_maximum_fusion.2.refs_0_), channel_id=1, source_target_pairs={{0,16},{1,5},{2,18},{3,7},{4,20},{5,1},{6,22},{7,3},{8,24},{9,13},... | collective-permute-start | bytes 786440 | tf_op jit(solution)/shard_map/ppermute | solution.py:48
  94.5 11.9 %collective-permute-start.24 = (bf16[4,128,256]{2,1,0:T(8,128)(2,1)S(1)}, bf16[4,128,256]{2,1,0:T(8,128)(2,1)S(1)}, u32[]{:S(2)}, u32[]{:S(2)}) collective-permute-start(bf16[4,128,256]{2,1,0:T(8,128)(2,1)S(1)} %pad_maximum_fusion.2.refs_0_), channel_id=1, source_target_pairs={{0,24},{1,7},{2,26},{3,1},{4,28},{5,3},{6,30},{7,5},{8,0},{9,15},{... | collective-permute-start | bytes 786440 | tf_op jit(solution)/shard_map/ppermute | solution.py:48
  94.6 12.6 %collective-permute-start.29 = (bf16[2,64,512]{2,1,0:T(8,128)(2,1)S(1)}, bf16[2,64,512]{2,1,0:T(8,128)(2,1)S(1)}, u32[]{:S(2)}, u32[]{:S(2)}) collective-permute-start(bf16[2,64,512]{2,1,0:T(8,128)(2,1)S(1)} %pad_maximum_fusion.6), channel_id=1, source_target_pairs={{0,32},{32,0},{64,96},{96,64},{1,33},{33,1},{65,97},{97,65},{2,34}... | collective-permute-start | bytes 393224 | tf_op jit(solution)/shard_map/ppermute | solution.py:56
  97.2 10.1 %collective-permute-start.25 = (bf16[256,256]{1,0:T(8,128)(2,1)S(1)}, bf16[256,256]{1,0:T(8,128)(2,1)S(1)}, u32[]{:S(2)}, u32[]{:S(2)}) collective-permute-start(bf16[256,256]{1,0:T(8,128)(2,1)S(1)} %copy-done.5), channel_id=1, source_target_pairs={{0,1},{1,0},{2,3},{3,2},{4,5},{5,4},{6,7},{7,6},{8,9},{9,8},{10,11... | collective-permute-start | bytes 393224 | tf_op jit(solution)/shard_map/ppermute | solution.py:52
  102.5 6.8 %collective-permute-start.30 = (bf16[4,128,256]{2,1,0:T(8,128)(2,1)S(1)}, bf16[4,128,256]{2,1,0:T(8,128)(2,1)S(1)}, u32[]{:S(2)}, u32[]{:S(2)}) collective-permute-start(bf16[4,128,256]{2,1,0:T(8,128)(2,1)S(1)} %pad_maximum_fusion.2.refs_0_), channel_id=1, source_target_pairs={{0,1},{1,0},{2,3},{3,2},{4,5},{5,4},{6,7},{7,6},{8,9},{9,8},{10,11... | collective-permute-start | bytes 786440 | tf_op jit(solution)/shard_map/ppermute | solution.py:52
  106.3 3.0 %collective-permute-start.32 = (bf16[4,128,256]{2,1,0:T(8,128)(2,1)S(1)}, bf16[4,128,256]{2,1,0:T(8,128)(2,1)S(1)}, u32[]{:S(2)}, u32[]{:S(2)}) collective-permute-start(bf16[4,128,256]{2,1,0:T(8,128)(2,1)S(1)} %collective-permute-done.23.refs_2_), channel_id=1, source_target_pairs={{0,1},{1,0},{2,3},{3,2},{4,5},{5,4},{6,7},{7,6},{8,9},{9,8},{10,11... | collective-permute-start | bytes 786440 | tf_op jit(solution)/shard_map/ppermute | solution.py:52
  (15 other events, 170.5 us)

commit v3 on v2

--- a/solution.py
+++ b/solution.py
@@ -118,7 +118,8 @@
 
 
 def project_up_kernel(place_ref, basis_ref, *refs):
-    grad_refs, before_ref, out_ref, sum_ref = refs[:8], refs[8:-2], refs[-2], refs[-1]
+    grad_refs, sum_ref = refs[:8], refs[-1]
+    before_ref, out_refs = (refs[8:9], refs[9:11]) if len(refs) > 10 else ((), refs[8:9])
     step = pl.program_id(0)
 
     @pl.when(step == 0)
@@ -138,7 +139,14 @@
 
     @pl.when(step == 1)
     def _():
-        out_ref[...] = sum_ref[...].astype(out_ref.dtype)
+        if not before_ref:
+            out_refs[0][...] = sum_ref[...]
+            return
+        z = place_ref[0]
+        for out_ref, first in zip(out_refs, (z ^ 1, z), strict=True):
+            for i, block in enumerate((first, 3 - first)):
+                rows = pl.ds(pl.multiple_of(block * 64, 64), 64)
+                out_ref[i] = sum_ref[rows, :].astype(out_ref.dtype)
 
 
 def project_up(place, basis, grad, own, before=None):
@@ -157,14 +165,20 @@
     if before is not None:
         in_specs.append(whole)
         operands.append(before)
+    if before is None:
+        out_shape, out_specs = jax.ShapeDtypeStruct((256, 512), f32), whole
+    else:
+        pair = pl.BlockSpec((2, 64, 512), lambda step, place: (0, 0, 0))
+        out_shape = [jax.ShapeDtypeStruct((2, 64, 512), t) for t in (bf16, f32)]
+        out_specs = [pair, pair]
     return pl.pallas_call(
         project_up_kernel,
-        out_shape=jax.ShapeDtypeStruct((256, 512), f32 if before is None else bf16),
+        out_shape=out_shape,
         grid_spec=pltpu.PrefetchScalarGridSpec(
             num_scalar_prefetch=1,
             grid=(2,),
             in_specs=in_specs,
-            out_specs=whole,
+            out_specs=out_specs,
             scratch_shapes=[pltpu.VMEM((256, 512), f32)],
         ),
         compiler_params=pltpu.CompilerParams(vmem_limit_bytes=60 << 20),
@@ -198,17 +212,24 @@
     )(place, own, *got)
 
 
-def norms_kernel(weights_ref, *refs):
+def basis_copies(place_ref, hbm_refs, refs, sems):
+    column = (place_ref[1] + 4 - place_ref[0]) % 4
+    return [
+        pltpu.make_async_copy(hbm_ref.at[:, column], ref, sems.at[i])
+        for i, (hbm_ref, ref) in enumerate(zip(hbm_refs, refs, strict=True))
+    ]
+
+
+def norms_kernel(place_ref, up_weight_ref, down_weight_ref, *refs):
     low_refs, (basis_down_ref, other_down_ref) = refs[:4], refs[4:6]
-    own_ref, other_ref, low_up_ref, out_ref = refs[6:]
+    own_hbm, other_hbm, low_up_ref, out_ref, own_ref, other_ref, sems = refs[6:]
+    copies = basis_copies(place_ref, (own_hbm, other_hbm), (own_ref, other_ref), sems)
+    for copy in copies:
+        copy.start()
 
     def square_sum(delta):
         return jnp.sum(jnp.sum(delta * delta, axis=0, keepdims=True), axis=1, keepdims=True)
 
-    up = jnp.zeros((1, 1), f32)
-    for ref in (own_ref, other_ref):
-        for block in range(4):
-            up += square_sum(jnp.dot(ref[block], low_up_ref[...], preferred_element_type=f32))
     down = jnp.zeros((1, 1), f32)
     for low_ref in low_refs:
         for ref in (basis_down_ref, other_down_ref):
@@ -220,20 +241,33 @@
                     preferred_element_type=f32,
                 )
             )
+    for copy in copies:
+        copy.wait()
+    up = jnp.zeros((1, 1), f32)
+    for ref in (own_ref, other_ref):
+        for block in range(4):
+            up += square_sum(jnp.dot(ref[block], low_up_ref[...], preferred_element_type=f32))
     lane = lax.broadcasted_iota(jnp.int32, (1, 128), 1)
-    row = jnp.where(lane == 0, weights_ref[0], weights_ref[1])
+    row = jnp.where(lane == 0, up_weight_ref[0], down_weight_ref[0])
     row = jnp.where(lane == 2, up, jnp.where(lane == 3, down, row))
     out_ref[...] = jnp.broadcast_to(row[None], out_ref.shape)
 
 
-def norms(weight_sums, lows, basis_down, other_down, own, other, low_up):
+def norms(place, up_weight, down_weight, lows, basis_down, other_down, own, other, low_up):
     vmem = pl.BlockSpec(memory_space=pltpu.VMEM)
-    operands = [weight_sums, *lows, basis_down, other_down, own, other, low_up]
+    smem = pl.BlockSpec(memory_space=pltpu.SMEM)
+    hbm = pl.BlockSpec(memory_space=pltpu.HBM)
+    operands = [place, up_weight, down_weight, *lows, basis_down, other_down, own, other, low_up]
     return pl.pallas_call(
         norms_kernel,
         out_shape=jax.ShapeDtypeStruct((128, 1, 128), f32),
-        in_specs=[pl.BlockSpec(memory_space=pltpu.SMEM)] + [vmem] * (len(operands) - 1),
+        in_specs=[smem] * 3 + [vmem] * 6 + [hbm] * 2 + [vmem],
         out_specs=vmem,
+        scratch_shapes=[
+            pltpu.VMEM((4, 256, 256), bf16),
+            pltpu.VMEM((4, 256, 256), bf16),
+            pltpu.SemaphoreType.DMA((2,)),
+        ],
         compiler_params=pltpu.CompilerParams(vmem_limit_bytes=16 << 20),
         cost_estimate=pl.CostEstimate(
             flops=1 << 34, bytes_accessed=3 << 20, transcendentals=0
@@ -243,9 +277,11 @@
 
 def update_kernel(place_ref, sums_ref, *refs):
     low_refs, (basis_down_ref, weight_down_ref) = refs[:8], refs[8:10]
-    own_ref, other_ref, low_up_hbm, weight_up_hbm, up_hbm, down_hbm = refs[10:16]
-    low_up_ref, weight_up_ref, up_ref, down_ref, in_sems, out_sems = refs[16:]
-    loads = [
+    own_hbm, other_hbm, low_up_hbm, weight_up_hbm, up_hbm, down_hbm = refs[10:16]
+    own_ref, other_ref, low_up_ref, weight_up_ref, up_ref, down_ref = refs[16:22]
+    in_sems, basis_sems, out_sems = refs[22:]
+    loads = basis_copies(place_ref, (own_hbm, other_hbm), (own_ref, other_ref), basis_sems)
+    loads += [
         pltpu.make_async_copy(low_up_hbm, low_up_ref, in_sems.at[0]),
         pltpu.make_async_copy(weight_up_hbm, weight_up_ref, in_sems.at[1]),
     ]
@@ -297,13 +333,16 @@
             jax.ShapeDtypeStruct(weight_up.shape, bf16),
             jax.ShapeDtypeStruct(weight_down.shape, bf16),
         ],
-        in_specs=[pl.BlockSpec(memory_space=pltpu.SMEM)] + [vmem] * (len(operands) - 3) + [hbm] * 2,
+        in_specs=[pl.BlockSpec(memory_space=pltpu.SMEM)] + [vmem] * (len(operands) - 5) + [hbm] * 4,
         out_specs=[hbm, hbm],
         scratch_shapes=[
+            pltpu.VMEM((4, 256, 256), bf16),
+            pltpu.VMEM((4, 256, 256), bf16),
             pltpu.VMEM(low_up.shape, bf16),
             pltpu.VMEM(weight_up.shape, bf16),
             pltpu.VMEM(weight_up.shape, bf16),
             pltpu.VMEM(weight_down.shape, bf16),
+            pltpu.SemaphoreType.DMA((2,)),
             pltpu.SemaphoreType.DMA((2,)),
             pltpu.SemaphoreType.DMA((5,)),
         ],
@@ -373,13 +412,9 @@
     other_basis_down = swap_cores(after(basis_down, two_own))
     partial_up = project_up(place, own_basis, local_up, True)
     two[0] = after(two[0], partial_up)
-    partial_up = project_up(place, other_basis, local_up, False, partial_up)
-    partial_up = partial_up.reshape(4, 64, 512)
-
-    mine, theirs = (z, 3 - z), (z ^ 1, 3 - (z ^ 1))
-    half_up = jnp.stack([pick(partial_up, block) for block in theirs])
-    half_up = exchange(half_up, 1).astype(f32)
-    half_up = half_up + jnp.stack([pick(partial_up, block) for block in mine]).astype(f32)
+
+    theirs, mine = project_up(place, other_basis, local_up, False, partial_up)
+    half_up = exchange(theirs, 1).astype(f32) + mine
 
     def part_three(k):
         index = (y + k) % 4
@@ -388,7 +423,7 @@
     three = [part_three(0)] + [
         shift(part_three(k).astype(bf16), "y", "y", k) for k in (2, 1, 3)
     ]
-    three[0] = after(three[0], partial_up)
+    three[0] = after(three[0], mine)
     proj_down = total(three[1:], three[0]) * (1.0 / replicas)
     new_moment_down, new_second_down, low_down = adam_update(proj_down, moment_down, second_down)
 
@@ -402,21 +437,19 @@
     ]
     all_low_up = jnp.stack([pick(all_up, at) for at in order]).reshape(256, 512)
 
-    blocks = [
-        lax.dynamic_index_in_dim(basis, (x + 4 - z) % 4, 1, keepdims=False)
-        for basis in (own_basis, other_basis)
-    ]
-
     inner = jnp.stack([low_down] + [shift(low_down, "y", "x", k) for k in (1, 2, 3)])
     outer = [inner] + [shift(inner, "x", "y", k) for k in (1, 2, 3)]
     sibling = [swap_cores(low) for low in outer]
 
     sums = norms(
-        jnp.stack([wsq_up, wsq_down]),
+        place,
+        wsq_up.reshape(1),
+        wsq_down.reshape(1),
         outer,
         basis_down,
         other_basis_down,
-        *blocks,
+        own_basis,
+        other_basis,
         all_low_up,
     )
     sums = after(sums, *sibling)
@@ -427,7 +460,8 @@
         outer + sibling,
         basis_down,
         weight_down.reshape(4, 4, 2, 128, 256),
-        *blocks,
+        own_basis,
+        other_basis,
         all_low_up,
         weight_up.reshape(4, 2, 256, 512),
     )

time: 132 us -> 128 us (0.970)
  waiting for transfers between devices: 20.8 us -> 28.4 us
  starting transfers between devices: 48.1 us -> 42.8 us
  blocking collectives: 18.4 us -> 14.7 us
  Pallas kernels: 24.4 us -> 27.6 us
  local copies, waits for them, and re-layouts: 7.53 us -> 4.45 us
  other arithmetic: 11.2 us -> 8.81 us
    ppermute x22, waiting for transfers between devices: 20.4 us -> 26 us  [shift(): return lax.ppermute(value, AXES, shift_pairs(axis0, axis1, k))]
    ppermute x22, starting transfers between devices: 31.1 us -> 26.2 us  [shift(): return lax.ppermute(value, AXES, shift_pairs(axis0, axis1, k))]
    all_to_all x1, blocking collectives: 18.4 us -> 14.7 us  [per_device(): sums = lax.all_to_all(sums, AXES, 0, 0, tiled=True)]
    pallas_call x1, Pallas kernels: 1.92 us -> 4.94 us  [norms(): pl.pallas_call(norms_kernel, out_shape=jax.ShapeDtypeStruct((128, 1, 128)...]
    squeeze x2 -> x0, local copies, waits for them, and re-layouts: 2.15 us -> none  [per_device(): lax.dynamic_index_in_dim(basis, (x + 4 - z) % 4, 1, keepdims=False)]
    another operation x2 -> x0, other arithmetic: 1.98 us -> none  [the longest x1 1.31 us: per_device(): jnp.stack([wsq_up, wsq_down])]
    ppermute x8, waiting for transfers between devices: 0.31 us -> 1.84 us  [swap_cores(): return lax.ppermute(value, 'c', [(0, 1), (1, 0)])]
    unnamed x26 -> x32, local copies, waits for them, and re-layouts: 4.35 us -> 4.37 us
  transfers between devices with their start and end apart: 34 -> 34, of which waited for: 11 -> 14; matrix products, arithmetic and copies ran while one was open for 10% -> 7% of each run, Pallas kernels for 12% -> 14%
where the time goes in v3:
time: 128 us
  starting transfers between devices  42.8 us (33%)
  waiting for transfers between devices  28.4 us (22%)
  Pallas kernels  27.6 us (22%)
  blocking collectives  14.7 us (11%)
  other arithmetic  8.81 us (7%)
  local copies, waits for them, and re-layouts  4.45 us (3%)
    ppermute x22, starting transfers between devices, shift(): return lax.ppermute(value, AXES, shift_pairs(axis0, axis1, k))  26.2 us
    ppermute x22, waiting for transfers between devices, shift(): return lax.ppermute(value, AXES, shift_pairs(axis0, axis1, k))  26 us
    ppermute x8, starting transfers between devices, swap_cores(): return lax.ppermute(value, 'c', [(0, 1), (1, 0)])  14.8 us
    all_to_all x1, blocking collectives, per_device(): sums = lax.all_to_all(sums, AXES, 0, 0, tiled=True)  14.7 us
    pallas_call x2, Pallas kernels, project_up(): pl.pallas_call(project_up_kernel, out_shape=out_shape, grid_spec=pltpu.Pr...  10.4 us
    pallas_call x6, Pallas kernels, project_rows(): pl.pallas_call(functools.partial(project_kernel, other is not None), out_...  7.32 us
    pallas_call x1, Pallas kernels, norms(): pl.pallas_call(norms_kernel, out_shape=jax.ShapeDtypeStruct((128, 1, 128)...  4.94 us
    unnamed x32, local copies, waits for them, and re-layouts  4.37 us
  transfers between devices with their start and end apart: 34, of which 14 were waited for; matrix products, arithmetic and copies ran while one was open for 7% of the time, Pallas kernels for 14%

profile of v3, /device:TPU:1, one launch (start us, length us, event | category | flops | bytes accessed | tf_op | source)
XLA Modules:
  0.0 127.9 jit_solution(7335272812259298612)
XLA Ops:
  0.7 3.4 %copy-done = bf16[1,16384,256]{2,1,0:T(8,128)(2,1)S(1)} copy-done((bf16[1,16384,256]{2,1,0:T(8,128)(2,1)S(1)}, bf16[1,16384,256]{2,1,0:T(8,128)(2,1)}, u32[]{:S(2)}) %copy-start) | copy-done | bytes 8388632
  6.0 1.5 %collective-permute-start = (bf16[1,4,4,128,256]{4,3,2,1,0:T(8,128)(2,1)S(1)}, bf16[1,4,4,128,256]{4,3,2,1,0:T(8,128)(2,1)S(1)}, u32[]{:S(2)}, u32[]{:S(2)}) collective-permute-start(bf16[1,4,4,128,256]{4,3,2,1,0:T(8,128)(2,1)S(1)} %shard_map.145), channel_id=1, source_target_pairs={{0,1},{1,0},{2,3},{3,2},{4,5},{5,4},{6,7},{7,6},{8,9},{9,8},{10,11... | collective-permute-start | bytes 3145736 | tf_op jit(solution)/shard_map/ppermute | solution.py:52
  10.2 1.6 %collective-permute-start.2 = (bf16[256,256]{1,0:T(8,128)(2,1)S(1)}, bf16[256,256]{1,0:T(8,128)(2,1)S(1)}, u32[]{:S(2)}, u32[]{:S(2)}) collective-permute-start(bf16[256,256]{1,0:T(8,128)(2,1)S(1)} %copy-done.15), channel_id=1, source_target_pairs={{0,16},{1,17},{2,18},{3,19},{4,20},{5,21},{6,22},{7,23},{8,24},{9,... | collective-permute-start | bytes 393224 | tf_op jit(solution)/shard_map/ppermute | solution.py:48
  11.8 2.0 %collective-permute-done.1 = bf16[256,256]{1,0:T(8,128)(2,1)S(1)} collective-permute-done((bf16[256,256]{1,0:T(8,128)(2,1)S(1)}, bf16[256,256]{1,0:T(8,128)(2,1)S(1)}, u32[]{:S(2)}, u32[]{:S(2)}) %collective-permute-start.1) | collective-permute-done | bytes 131104 | tf_op jit(solution)/shard_map/ppermute | solution.py:48
  13.8 3.9 %collective-permute-done.2 = bf16[256,256]{1,0:T(8,128)(2,1)S(1)} collective-permute-done((bf16[256,256]{1,0:T(8,128)(2,1)S(1)}, bf16[256,256]{1,0:T(8,128)(2,1)S(1)}, u32[]{:S(2)}, u32[]{:S(2)}) %collective-permute-start.2) | collective-permute-done | bytes 131104 | tf_op jit(solution)/shard_map/ppermute | solution.py:48
  18.7 2.4 %shard_map.147 = bf16[3,4,4,128,256]{4,3,2,1,0:T(8,128)(2,1)S(1)} custom-call(s32[4]{0:T(128)S(1)} %pad_add_fusion.place_ref, bf16[4,4,4,2,128,256]{5,4,3,2,1,0:T(8,128)(2,1)S(1)} %bitcast.63, bf16[4,4,4,2,128,256]{5,4,3,2,1,0:T(8,128)(2,1)S(1)} %bitcast.61, bf16[4,4,4,2,128,256]{5,4,3,2,1,0:T(8,128)(2,1)S(1)} %bitcast.62, ...), custom_call_target="tpu_custom_call" | custom-call | flops 3 | bytes 3 | tf_op jit(solution)/shard_map/pallas_call | solution.py:104
  22.1 2.7 %collective-permute-start.10 = (bf16[4,256,256]{2,1,0:T(8,128)(2,1)S(1)}, bf16[4,256,256]{2,1,0:T(8,128)(2,1)S(1)}, u32[]{:S(2)}, u32[]{:S(2)}) collective-permute-start(bf16[4,256,256]{2,1,0:T(8,128)(2,1)S(1)} %pad_maximum_fusion.1), channel_id=1, source_target_pairs={{0,6},{1,7},{2,0},{3,1},{4,2},{5,3},{6,4},{7,5},{8,14},{9,15},{10,... | collective-permute-start | bytes 1572872 | tf_op jit(solution)/shard_map/ppermute | solution.py:48
  25.6 1.8 %collective-permute-done.4.refs_5_ = bf16[3,4,4,128,256]{4,3,2,1,0:T(8,128)(2,1)S(1)} collective-permute-done((bf16[3,4,4,128,256]{4,3,2,1,0:T(8,128)(2,1)S(1)}, bf16[3,4,4,128,256]{4,3,2,1,0:T(8,128)(2,1)S(1)}, u32[]{:S(2)}, u32[]{:S(2)}) %collective-permute-start.4) | collective-permute-done | bytes 3145760 | tf_op jit(solution)/shard_map/ppermute | solution.py:52
  29.3 1.7 %collective-permute-start.7 = (bf16[4,4,128,256]{3,2,1,0:T(8,128)(2,1)S(1)}, bf16[4,4,128,256]{3,2,1,0:T(8,128)(2,1)S(1)}, u32[]{:S(2)}, u32[]{:S(2)}) collective-permute-start(bf16[4,4,128,256]{3,2,1,0:T(8,128)(2,1)S(1)} %bitcast.81), channel_id=1, source_target_pairs={{0,96},{1,25},{2,98},{3,27},{4,100},{5,29},{6,102},{7,31},{8,104},... | collective-permute-start | bytes 3145736 | tf_op jit(solution)/shard_map/ppermute | solution.py:48
  31.0 5.1 %collective-permute-done.10 = bf16[4,256,256]{2,1,0:T(8,128)(2,1)S(1)} collective-permute-done((bf16[4,256,256]{2,1,0:T(8,128)(2,1)S(1)}, bf16[4,256,256]{2,1,0:T(8,128)(2,1)S(1)}, u32[]{:S(2)}, u32[]{:S(2)}) %collective-permute-start.10) | collective-permute-done | bytes 524320 | tf_op jit(solution)/shard_map/ppermute | solution.py:48
  36.1 3.1 %collective-permute-done.8 = bf16[4,256,256]{2,1,0:T(8,128)(2,1)S(1)} collective-permute-done((bf16[4,256,256]{2,1,0:T(8,128)(2,1)S(1)}, bf16[4,256,256]{2,1,0:T(8,128)(2,1)S(1)}, u32[]{:S(2)}, u32[]{:S(2)}) %collective-permute-start.8) | collective-permute-done | bytes 524320 | tf_op jit(solution)/shard_map/ppermute | solution.py:48
  40.3 2.7 %collective-permute-start.11 = (bf16[2,256,256]{2,1,0:T(8,128)(2,1)S(1)}, bf16[2,256,256]{2,1,0:T(8,128)(2,1)S(1)}, u32[]{:S(2)}, u32[]{:S(2)}) collective-permute-start(bf16[2,256,256]{2,1,0:T(8,128)(2,1)S(1)} %slice.18), channel_id=1, source_target_pairs={{0,6},{1,7},{2,0},{3,1},{4,2},{5,3},{6,4},{7,5},{8,14},{9,15},{10,... | collective-permute-start | bytes 786440 | tf_op jit(solution)/shard_map/ppermute | solution.py:48
  43.0 1.7 %multiply_reduce_fusion = f32[]{:T(128)} fusion(bf16[4096,256]{1,0:T(8,128)(2,1)S(1)} %copy-done.5), kind=kLoop, calls=%fused_computation | loop fusion | flops 3145727 | bytes 2097156 | tf_op jit(solution)/shard_map/reduce_sum | solution.py:387
  44.7 1.7 %multiply_reduce_fusion.1 = f32[]{:T(128)} fusion(bf16[2048,512]{1,0:T(8,128)(2,1)S(1)} %copy-done.3), kind=kLoop, calls=%fused_computation.1 | loop fusion | flops 3145727 | bytes 2097156 | tf_op jit(solution)/shard_map/reduce_sum | solution.py:386
  46.5 1.7 %collective-permute-done.9 = bf16[2,256,256]{2,1,0:T(8,128)(2,1)S(1)} collective-permute-done((bf16[2,256,256]{2,1,0:T(8,128)(2,1)S(1)}, bf16[2,256,256]{2,1,0:T(8,128)(2,1)S(1)}, u32[]{:S(2)}, u32[]{:S(2)}) %collective-permute-start.9) | collective-permute-done | bytes 262176 | tf_op jit(solution)/shard_map/ppermute | solution.py:48
  48.2 2.7 %collective-permute-done.7.refs_2_ = bf16[4,4,128,256]{3,2,1,0:T(8,128)(2,1)S(1)} collective-permute-done((bf16[4,4,128,256]{3,2,1,0:T(8,128)(2,1)S(1)}, bf16[4,4,128,256]{3,2,1,0:T(8,128)(2,1)S(1)}, u32[]{:S(2)}, u32[]{:S(2)}) %collective-permute-start.7) | collective-permute-done | bytes 1048608 | tf_op jit(solution)/shard_map/ppermute | solution.py:48
  52.9 2.7 %collective-permute-start.15 = (bf16[4,4,256,256]{3,2,1,0:T(8,128)(2,1)S(1)}, bf16[4,4,256,256]{3,2,1,0:T(8,128)(2,1)}, u32[]{:S(2)}, u32[]{:S(2)}) collective-permute-start(bf16[4,4,256,256]{3,2,1,0:T(8,128)(2,1)S(1)} %pad_maximum_fusion.basis_ref.refs_6_.refs_10_), channel_id=1, source_target_pairs={{0,1},{1,0},{2,3},{3,2},{4,5},{5,4},{6,7},{7,6},{8,9},{9,8},{10,11... | collective-permute-start | bytes 6291464 | tf_op jit(solution)/shard_map/ppermute | solution.py:52
  55.6 2.2 %collective-permute-start.12 = (bf16[4,128,256]{2,1,0:T(8,128)(2,1)S(1)}, bf16[4,128,256]{2,1,0:T(8,128)(2,1)}, u32[]{:S(2)}, u32[]{:S(2)}) collective-permute-start(bf16[4,128,256]{2,1,0:T(8,128)(2,1)S(1)} %get-tuple-element.34), channel_id=1, source_target_pairs={{0,16},{1,65},{2,18},{3,67},{4,20},{5,69},{6,22},{7,71},{8,24},{9,... | collective-permute-start | bytes 786440 | tf_op jit(solution)/shard_map/ppermute | solution.py:48
  58.5 1.9 %collective-permute-start.14 = (bf16[4,128,256]{2,1,0:T(8,128)(2,1)S(1)}, bf16[4,128,256]{2,1,0:T(8,128)(2,1)}, u32[]{:S(2)}, u32[]{:S(2)}) collective-permute-start(bf16[4,128,256]{2,1,0:T(8,128)(2,1)S(1)} %get-tuple-element.36), channel_id=1, source_target_pairs={{0,24},{1,97},{2,26},{3,99},{4,28},{5,101},{6,30},{7,103},{8,0},{9... | collective-permute-start | bytes 786440 | tf_op jit(solution)/shard_map/ppermute | solution.py:48
  60.4 5.1 %shard_map.152.refs_8_ = f32[256,512]{1,0:T(8,128)} custom-call(s32[4]{0:T(128)} %copy-done.9, bf16[4,4,256,256]{3,2,1,0:T(8,128)(2,1)} %copy-done.1, bf16[8192,512]{1,0:T(8,128)(2,1)} %bitcast.84, bf16[8192,512]{1,0:T(8,128)(2,1)} %bitcast.85, bf16[8192,512]{1,0:T(8,128)(2,1)} %bitcast.86, bf16[8192,512]{1,0:T(8,128)(2,1)} %bitcast.87, ...), custom_call_target="tpu_custom_call" | custom-call | flops 1 | bytes 1 | tf_op jit(solution)/shard_map/pallas_call | solution.py:174
  65.6 5.3 %shard_map.153 = (bf16[2,64,512]{2,1,0:T(8,128)(2,1)}, f32[2,64,512]{2,1,0:T(8,128)}) custom-call(s32[4]{0:T(128)} %copy-done.9, bf16[4,4,256,256]{3,2,1,0:T(8,128)(2,1)} %collective-permute-done.15.basis_ref.refs_7_.refs_11_, bf16[8192,512]{1,0:T(8,128)(2,1)} %bitcast.92, bf16[8192,512]{1,0:T(8,128)(2,1)} %bitcast.93, bf16[8192,512]{1,0:T(8,128)(2,1)} %bitcast.94, ...), custom_call_target="tpu_custom_call" | custom-call | flops 1 | bytes 1 | tf_op jit(solution)/shard_map/pallas_call | solution.py:174
  72.5 2.0 %collective-permute-start.16 = (bf16[128,256]{1,0:T(8,128)(2,1)S(1)}, bf16[128,256]{1,0:T(8,128)(2,1)S(1)}, u32[]{:S(2)}, u32[]{:S(2)}) collective-permute-start(bf16[128,256]{1,0:T(8,128)(2,1)S(1)} %get-tuple-element.50), channel_id=1, source_target_pairs={{0,4},{1,5},{2,6},{3,7},{4,0},{5,1},{6,2},{7,3},{8,12},{9,13},{10,... | collective-permute-start | bytes 196616 | tf_op jit(solution)/shard_map/ppermute | solution.py:48
  80.8 1.7 %collective-permute-start.21 = (bf16[128,256]{1,0:T(8,128)(2,1)S(1)}, bf16[128,256]{1,0:T(8,128)(2,1)S(1)}, u32[]{:S(2)}, u32[]{:S(2)}) collective-permute-start(bf16[128,256]{1,0:T(8,128)(2,1)S(1)} %get-tuple-element.47), channel_id=1, source_target_pairs={{0,6},{1,25},{2,0},{3,27},{4,2},{5,29},{6,4},{7,31},{8,14},{9,1},{... | collective-permute-start | bytes 196616 | tf_op jit(solution)/shard_map/ppermute | solution.py:48
  84.7 2.5 %collective-permute-done.20 = bf16[128,256]{1,0:T(8,128)(2,1)S(1)} collective-permute-done((bf16[128,256]{1,0:T(8,128)(2,1)S(1)}, bf16[128,256]{1,0:T(8,128)(2,1)S(1)}, u32[]{:S(2)}, u32[]{:S(2)}) %collective-permute-start.20) | collective-permute-done | bytes 65568 | tf_op jit(solution)/shard_map/ppermute | solution.py:48
  88.2 1.8 %collective-permute-start.24 = (bf16[4,128,256]{2,1,0:T(8,128)(2,1)S(1)}, bf16[4,128,256]{2,1,0:T(8,128)(2,1)S(1)}, u32[]{:S(2)}, u32[]{:S(2)}) collective-permute-start(bf16[4,128,256]{2,1,0:T(8,128)(2,1)S(1)} %pad_maximum_fusion.2.refs_0_), channel_id=1, source_target_pairs={{0,24},{1,7},{2,26},{3,1},{4,28},{5,3},{6,30},{7,5},{8,0},{9,15},{... | collective-permute-start | bytes 786440 | tf_op jit(solution)/shard_map/ppermute | solution.py:48
  90.7 1.5 %collective-permute-start.29 = (bf16[2,64,512]{2,1,0:T(8,128)(2,1)S(1)}, bf16[2,64,512]{2,1,0:T(8,128)(2,1)}, u32[]{:S(2)}, u32[]{:S(2)}) collective-permute-start(bf16[2,64,512]{2,1,0:T(8,128)(2,1)S(1)} %pad_maximum_fusion.5), channel_id=1, source_target_pairs={{0,32},{32,0},{64,96},{96,64},{1,33},{33,1},{65,97},{97,65},{2,34}... | collective-permute-start | bytes 393224 | tf_op jit(solution)/shard_map/ppermute | solution.py:56
  92.2 2.7 %collective-permute-start.25 = (bf16[256,256]{1,0:T(8,128)(2,1)S(1)}, bf16[256,256]{1,0:T(8,128)(2,1)S(1)}, u32[]{:S(2)}, u32[]{:S(2)}) collective-permute-start(bf16[256,256]{1,0:T(8,128)(2,1)S(1)} %copy-done.8), channel_id=1, source_target_pairs={{0,1},{1,0},{2,3},{3,2},{4,5},{5,4},{6,7},{7,6},{8,9},{9,8},{10,11... | collective-permute-start | bytes 393224 | tf_op jit(solution)/shard_map/ppermute | solution.py:52
  97.1 3.3 %collective-permute-start.33 = (bf16[4,128,256]{2,1,0:T(8,128)(2,1)S(1)}, bf16[4,128,256]{2,1,0:T(8,128)(2,1)S(1)}, u32[]{:S(2)}, u32[]{:S(2)}) collective-permute-start(bf16[4,128,256]{2,1,0:T(8,128)(2,1)S(1)} %collective-permute-done.24.refs_3_), channel_id=1, source_target_pairs={{0,1},{1,0},{2,3},{3,2},{4,5},{5,4},{6,7},{7,6},{8,9},{9,8},{10,11... | collective-permute-start | bytes 786440 | tf_op jit(solution)/shard_map/ppermute | solution.py:52
  100.4 2.7 %collective-permute-start.32 = (bf16[4,128,256]{2,1,0:T(8,128)(2,1)S(1)}, bf16[4,128,256]{2,1,0:T(8,128)(2,1)S(1)}, u32[]{:S(2)}, u32[]{:S(2)}) collective-permute-start(bf16[4,128,256]{2,1,0:T(8,128)(2,1)S(1)} %collective-permute-done.23.refs_2_), channel_id=1, source_target_pairs={{0,1},{1,0},{2,3},{3,2},{4,5},{5,4},{6,7},{7,6},{8,9},{9,8},{10,11... | collective-permute-start | bytes 786440 | tf_op jit(solution)/shard_map/ppermute | solution.py:52
  104.2 4.9 %shard_map.154 = f32[128,1,128]{2,1,0:T(1,128)S(1)} custom-call(s32[4]{0:T(128)S(1)} %copy-done.10, f32[1]{0:T(128)} %bitcast.4.up_weight_ref, f32[1]{0:T(128)} %bitcast.5.down_weight_ref, bf16[4,128,256]{2,1,0:T(8,128)(2,1)S(1)} %pad_maximum_fusion.2.refs_0_, bf16[4,128,256]{2,1,0:T(8,128)(2,1)S(1)} %collective-permute-done.22.refs_1_, ...), custom_call_target="tpu_custom_call" | custom-call | flops 17179869184 | bytes 3145728 | tf_op jit(solution)/shard_map/pallas_call | solution.py:261
  109.2 14.7 %all_to_all.5.sums_ref = f32[128,1,128]{2,1,0:T(1,128)S(1)} all-to-all(f32[128,1,128]{2,1,0:T(1,128)S(1)} %shard_map.154), channel_id=1, replica_groups=mesh['z'=4,'x'=4,'y'=4,'c'=2] {'z','x','y','c'}, dimensions={0} | all-to-all | bytes 131072 | tf_op jit(solution)/shard_map/all_to_all | solution.py:456
  123.9 3.9 %shard_map.155 = (bf16[4,2,256,512]{3,2,1,0:T(8,128)(2,1)}, bf16[4,4,2,128,256]{4,3,2,1,0:T(8,128)(2,1)}) custom-call(s32[4]{0:T(128)S(1)} %copy-done.10, f32[128,1,128]{2,1,0:T(1,128)S(1)} %all_to_all.5.sums_ref, bf16[4,128,256]{2,1,0:T(8,128)(2,1)S(1)} %pad_maximum_fusion.2.refs_0_, bf16[4,128,256]{2,1,0:T(8,128)(2,1)S(1)} %collective-permute-done.22.refs_1_, ...), custom_call_target="tpu_custom_call" | custom-call | flops 1073741824 | bytes 11534336 | tf_op jit(solution)/shard_map/pallas_call | solution.py:330
  (98 shorter events, 28.2 us)
Async XLA Ops:
  6.0 11.7 %collective-permute-start = (bf16[1,4,4,128,256]{4,3,2,1,0:T(8,128)(2,1)S(1)}, bf16[1,4,4,128,256]{4,3,2,1,0:T(8,128)(2,1)S(1)}, u32[]{:S(2)}, u32[]{:S(2)}) collective-permute-start(bf16[1,4,4,128,256]{4,3,2,1,0:T(8,128)(2,1)S(1)} %shard_map.145), channel_id=1, source_target_pairs={{0,1},{1,0},{2,3},{3,2},{4,5},{5,4},{6,7},{7,6},{8,9},{9,8},{10,11... | collective-permute-start | bytes 3145736 | tf_op jit(solution)/shard_map/ppermute | solution.py:52
  7.5 6.3 %collective-permute-start.1 = (bf16[256,256]{1,0:T(8,128)(2,1)S(1)}, bf16[256,256]{1,0:T(8,128)(2,1)S(1)}, u32[]{:S(2)}, u32[]{:S(2)}) collective-permute-start(bf16[256,256]{1,0:T(8,128)(2,1)S(1)} %copy-done.15), channel_id=1, source_target_pairs={{0,8},{1,9},{2,10},{3,11},{4,12},{5,13},{6,14},{7,15},{8,16},{9,17... | collective-permute-start | bytes 393224 | tf_op jit(solution)/shard_map/ppermute | solution.py:48
  8.8 5.0 %collective-permute-start.3 = (bf16[256,256]{1,0:T(8,128)(2,1)S(1)}, bf16[256,256]{1,0:T(8,128)(2,1)S(1)}, u32[]{:S(2)}, u32[]{:S(2)}) collective-permute-start(bf16[256,256]{1,0:T(8,128)(2,1)S(1)} %copy-done.15), channel_id=1, source_target_pairs={{0,24},{1,25},{2,26},{3,27},{4,28},{5,29},{6,30},{7,31},{8,0},{9,1... | collective-permute-start | bytes 393224 | tf_op jit(solution)/shard_map/ppermute | solution.py:48
  10.2 7.5 %collective-permute-start.2 = (bf16[256,256]{1,0:T(8,128)(2,1)S(1)}, bf16[256,256]{1,0:T(8,128)(2,1)S(1)}, u32[]{:S(2)}, u32[]{:S(2)}) collective-permute-start(bf16[256,256]{1,0:T(8,128)(2,1)S(1)} %copy-done.15), channel_id=1, source_target_pairs={{0,16},{1,17},{2,18},{3,19},{4,20},{5,21},{6,22},{7,23},{8,24},{9,... | collective-permute-start | bytes 393224 | tf_op jit(solution)/shard_map/ppermute | solution.py:48
  21.2 6.2 %collective-permute-start.4 = (bf16[3,4,4,128,256]{4,3,2,1,0:T(8,128)(2,1)S(1)}, bf16[3,4,4,128,256]{4,3,2,1,0:T(8,128)(2,1)S(1)}, u32[]{:S(2)}, u32[]{:S(2)}) collective-permute-start(bf16[3,4,4,128,256]{4,3,2,1,0:T(8,128)(2,1)S(1)} %shard_map.147), channel_id=1, source_target_pairs={{0,1},{1,0},{2,3},{3,2},{4,5},{5,4},{6,7},{7,6},{8,9},{9,8},{10,11... | collective-permute-start | bytes 9437192 | tf_op jit(solution)/shard_map/ppermute | solution.py:52
  22.1 14.0 %collective-permute-start.10 = (bf16[4,256,256]{2,1,0:T(8,128)(2,1)S(1)}, bf16[4,256,256]{2,1,0:T(8,128)(2,1)S(1)}, u32[]{:S(2)}, u32[]{:S(2)}) collective-permute-start(bf16[4,256,256]{2,1,0:T(8,128)(2,1)S(1)} %pad_maximum_fusion.1), channel_id=1, source_target_pairs={{0,6},{1,7},{2,0},{3,1},{4,2},{5,3},{6,4},{7,5},{8,14},{9,15},{10,... | collective-permute-start | bytes 1572872 | tf_op jit(solution)/shard_map/ppermute | solution.py:48
  24.8 14.4 %collective-permute-start.8 = (bf16[4,256,256]{2,1,0:T(8,128)(2,1)S(1)}, bf16[4,256,256]{2,1,0:T(8,128)(2,1)S(1)}, u32[]{:S(2)}, u32[]{:S(2)}) collective-permute-start(bf16[4,256,256]{2,1,0:T(8,128)(2,1)S(1)} %pad_maximum_fusion.1), channel_id=1, source_target_pairs={{0,2},{1,3},{2,4},{3,5},{4,6},{5,7},{6,0},{7,1},{8,10},{9,11},{10,... | collective-permute-start | bytes 1572872 | tf_op jit(solution)/shard_map/ppermute | solution.py:48
  24.9 23.4 %collective-permute-start.5 = (bf16[4,4,128,256]{3,2,1,0:T(8,128)(2,1)S(1)}, bf16[4,4,128,256]{3,2,1,0:T(8,128)(2,1)S(1)}, u32[]{:S(2)}, u32[]{:S(2)}) collective-permute-start(bf16[4,4,128,256]{3,2,1,0:T(8,128)(2,1)S(1)} %bitcast.79), channel_id=1, source_target_pairs={{0,64},{1,17},{2,66},{3,19},{4,68},{5,21},{6,70},{7,23},{8,72},{9,... | collective-permute-start | bytes 3145736 | tf_op jit(solution)/shard_map/ppermute | solution.py:48
  29.3 21.5 %collective-permute-start.7 = (bf16[4,4,128,256]{3,2,1,0:T(8,128)(2,1)S(1)}, bf16[4,4,128,256]{3,2,1,0:T(8,128)(2,1)S(1)}, u32[]{:S(2)}, u32[]{:S(2)}) collective-permute-start(bf16[4,4,128,256]{3,2,1,0:T(8,128)(2,1)S(1)} %bitcast.81), channel_id=1, source_target_pairs={{0,96},{1,25},{2,98},{3,27},{4,100},{5,29},{6,102},{7,31},{8,104},... | collective-permute-start | bytes 3145736 | tf_op jit(solution)/shard_map/ppermute | solution.py:48
  31.0 20.5 %collective-permute-start.6 = (bf16[4,4,128,256]{3,2,1,0:T(8,128)(2,1)S(1)}, bf16[4,4,128,256]{3,2,1,0:T(8,128)(2,1)S(1)}, u32[]{:S(2)}, u32[]{:S(2)}) collective-permute-start(bf16[4,4,128,256]{3,2,1,0:T(8,128)(2,1)S(1)} %bitcast.80), channel_id=1, source_target_pairs={{0,32},{1,9},{2,34},{3,11},{4,36},{5,13},{6,38},{7,15},{8,40},{9,1... | collective-permute-start | bytes 3145736 | tf_op jit(solution)/shard_map/ppermute | solution.py:48
  40.2 7.9 %collective-permute-start.9 = (bf16[2,256,256]{2,1,0:T(8,128)(2,1)S(1)}, bf16[2,256,256]{2,1,0:T(8,128)(2,1)S(1)}, u32[]{:S(2)}, u32[]{:S(2)}) collective-permute-start(bf16[2,256,256]{2,1,0:T(8,128)(2,1)S(1)} %slice.17), channel_id=1, source_target_pairs={{0,2},{1,3},{2,4},{3,5},{4,6},{5,7},{6,0},{7,1},{8,10},{9,11},{10,... | collective-permute-start | bytes 786440 | tf_op jit(solution)/shard_map/ppermute | solution.py:48
  40.3 7.8 %collective-permute-start.11 = (bf16[2,256,256]{2,1,0:T(8,128)(2,1)S(1)}, bf16[2,256,256]{2,1,0:T(8,128)(2,1)S(1)}, u32[]{:S(2)}, u32[]{:S(2)}) collective-permute-start(bf16[2,256,256]{2,1,0:T(8,128)(2,1)S(1)} %slice.18), channel_id=1, source_target_pairs={{0,6},{1,7},{2,0},{3,1},{4,2},{5,3},{6,4},{7,5},{8,14},{9,15},{10,... | collective-permute-start | bytes 786440 | tf_op jit(solution)/shard_map/ppermute | solution.py:48
  52.9 12.7 %collective-permute-start.15 = (bf16[4,4,256,256]{3,2,1,0:T(8,128)(2,1)S(1)}, bf16[4,4,256,256]{3,2,1,0:T(8,128)(2,1)}, u32[]{:S(2)}, u32[]{:S(2)}) collective-permute-start(bf16[4,4,256,256]{3,2,1,0:T(8,128)(2,1)S(1)} %pad_maximum_fusion.basis_ref.refs_6_.refs_10_), channel_id=1, source_target_pairs={{0,1},{1,0},{2,3},{3,2},{4,5},{5,4},{6,7},{7,6},{8,9},{9,8},{10,11... | collective-permute-start | bytes 6291464 | tf_op jit(solution)/shard_map/ppermute | solution.py:52
  55.6 15.6 %collective-permute-start.12 = (bf16[4,128,256]{2,1,0:T(8,128)(2,1)S(1)}, bf16[4,128,256]{2,1,0:T(8,128)(2,1)}, u32[]{:S(2)}, u32[]{:S(2)}) collective-permute-start(bf16[4,128,256]{2,1,0:T(8,128)(2,1)S(1)} %get-tuple-element.34), channel_id=1, source_target_pairs={{0,16},{1,65},{2,18},{3,67},{4,20},{5,69},{6,22},{7,71},{8,24},{9,... | collective-permute-start | bytes 786440 | tf_op jit(solution)/shard_map/ppermute | solution.py:48
  57.8 13.5 %collective-permute-start.13 = (bf16[4,128,256]{2,1,0:T(8,128)(2,1)S(1)}, bf16[4,128,256]{2,1,0:T(8,128)(2,1)}, u32[]{:S(2)}, u32[]{:S(2)}) collective-permute-start(bf16[4,128,256]{2,1,0:T(8,128)(2,1)S(1)} %get-tuple-element.35), channel_id=1, source_target_pairs={{0,8},{1,33},{2,10},{3,35},{4,12},{5,37},{6,14},{7,39},{8,16},{9,4... | collective-permute-start | bytes 786440 | tf_op jit(solution)/shard_map/ppermute | solution.py:48
  58.5 12.7 %collective-permute-start.14 = (bf16[4,128,256]{2,1,0:T(8,128)(2,1)S(1)}, bf16[4,128,256]{2,1,0:T(8,128)(2,1)}, u32[]{:S(2)}, u32[]{:S(2)}) collective-permute-start(bf16[4,128,256]{2,1,0:T(8,128)(2,1)S(1)} %get-tuple-element.36), channel_id=1, source_target_pairs={{0,24},{1,97},{2,26},{3,99},{4,28},{5,101},{6,30},{7,103},{8,0},{9... | collective-permute-start | bytes 786440 | tf_op jit(solution)/shard_map/ppermute | solution.py:48
  70.9 5.8 %collective-permute-start.26 = (bf16[2,64,512]{2,1,0:T(8,128)(2,1)}, bf16[2,64,512]{2,1,0:T(8,128)(2,1)S(1)}, u32[]{:S(2)}, u32[]{:S(2)}) collective-permute-start(bf16[2,64,512]{2,1,0:T(8,128)(2,1)} %get-tuple-element.40), channel_id=1, source_target_pairs={{0,32},{32,0},{64,96},{96,64},{1,33},{33,1},{65,97},{97,65},{2,34}... | collective-permute-start | bytes 393224 | tf_op jit(solution)/shard_map/ppermute | solution.py:56
  72.5 5.3 %collective-permute-start.16 = (bf16[128,256]{1,0:T(8,128)(2,1)S(1)}, bf16[128,256]{1,0:T(8,128)(2,1)S(1)}, u32[]{:S(2)}, u32[]{:S(2)}) collective-permute-start(bf16[128,256]{1,0:T(8,128)(2,1)S(1)} %get-tuple-element.50), channel_id=1, source_target_pairs={{0,4},{1,5},{2,6},{3,7},{4,0},{5,1},{6,2},{7,3},{8,12},{9,13},{10,... | collective-permute-start | bytes 196616 | tf_op jit(solution)/shard_map/ppermute | solution.py:48
  74.5 4.5 %collective-permute-start.18 = (bf16[128,256]{1,0:T(8,128)(2,1)S(1)}, bf16[128,256]{1,0:T(8,128)(2,1)S(1)}, u32[]{:S(2)}, u32[]{:S(2)}) collective-permute-start(bf16[128,256]{1,0:T(8,128)(2,1)S(1)} %get-tuple-element.51), channel_id=1, source_target_pairs={{0,6},{1,7},{2,0},{3,1},{4,2},{5,3},{6,4},{7,5},{8,14},{9,15},{10,... | collective-permute-start | bytes 196616 | tf_op jit(solution)/shard_map/ppermute | solution.py:48
  75.7 4.3 %collective-permute-start.17 = (bf16[128,256]{1,0:T(8,128)(2,1)S(1)}, bf16[128,256]{1,0:T(8,128)(2,1)S(1)}, u32[]{:S(2)}, u32[]{:S(2)}) collective-permute-start(bf16[128,256]{1,0:T(8,128)(2,1)S(1)} %get-tuple-element.52), channel_id=1, source_target_pairs={{0,2},{1,3},{2,4},{3,5},{4,6},{5,7},{6,0},{7,1},{8,10},{9,11},{10,... | collective-permute-start | bytes 196616 | tf_op jit(solution)/shard_map/ppermute | solution.py:48
  77.7 6.1 %collective-permute-start.27 = (bf16[64,512]{1,0:T(8,128)(2,1)S(1)}, bf16[64,512]{1,0:T(8,128)(2,1)S(1)}, u32[]{:S(2)}, u32[]{:S(2)}) collective-permute-start(bf16[64,512]{1,0:T(8,128)(2,1)S(1)} %fusion.4), channel_id=1, source_target_pairs={{0,96},{32,64},{64,32},{96,0},{1,97},{33,65},{65,33},{97,1},{2,98}... | collective-permute-start | bytes 196616 | tf_op jit(solution)/shard_map/ppermute | solution.py:56
  82.5 4.6 %collective-permute-start.20 = (bf16[128,256]{1,0:T(8,128)(2,1)S(1)}, bf16[128,256]{1,0:T(8,128)(2,1)S(1)}, u32[]{:S(2)}, u32[]{:S(2)}) collective-permute-start(bf16[128,256]{1,0:T(8,128)(2,1)S(1)} %get-tuple-element.47), channel_id=1, source_target_pairs={{0,4},{1,17},{2,6},{3,19},{4,0},{5,21},{6,2},{7,23},{8,12},{9,25},... | collective-permute-start | bytes 196616 | tf_op jit(solution)/shard_map/ppermute | solution.py:48
  84.7 6.0 %collective-permute-start.28 = (bf16[64,512]{1,0:T(8,128)(2,1)S(1)}, bf16[64,512]{1,0:T(8,128)(2,1)S(1)}, u32[]{:S(2)}, u32[]{:S(2)}) collective-permute-start(bf16[64,512]{1,0:T(8,128)(2,1)S(1)} %get-tuple-element.44), channel_id=1, source_target_pairs={{0,96},{32,64},{64,32},{96,0},{1,97},{33,65},{65,33},{97,1},{2,98}... | collective-permute-start | bytes 196616 | tf_op jit(solution)/shard_map/ppermute | solution.py:56
  88.2 7.9 %collective-permute-start.24 = (bf16[4,128,256]{2,1,0:T(8,128)(2,1)S(1)}, bf16[4,128,256]{2,1,0:T(8,128)(2,1)S(1)}, u32[]{:S(2)}, u32[]{:S(2)}) collective-permute-start(bf16[4,128,256]{2,1,0:T(8,128)(2,1)S(1)} %pad_maximum_fusion.2.refs_0_), channel_id=1, source_target_pairs={{0,24},{1,7},{2,26},{3,1},{4,28},{5,3},{6,30},{7,5},{8,0},{9,15},{... | collective-permute-start | bytes 786440 | tf_op jit(solution)/shard_map/ppermute | solution.py:48
  90.0 7.1 %collective-permute-start.23 = (bf16[4,128,256]{2,1,0:T(8,128)(2,1)S(1)}, bf16[4,128,256]{2,1,0:T(8,128)(2,1)S(1)}, u32[]{:S(2)}, u32[]{:S(2)}) collective-permute-start(bf16[4,128,256]{2,1,0:T(8,128)(2,1)S(1)} %pad_maximum_fusion.2.refs_0_), channel_id=1, source_target_pairs={{0,16},{1,5},{2,18},{3,7},{4,20},{5,1},{6,22},{7,3},{8,24},{9,13},... | collective-permute-start | bytes 786440 | tf_op jit(solution)/shard_map/ppermute | solution.py:48
  90.0 10.4 %collective-permute-start.22 = (bf16[4,128,256]{2,1,0:T(8,128)(2,1)S(1)}, bf16[4,128,256]{2,1,0:T(8,128)(2,1)S(1)}, u32[]{:S(2)}, u32[]{:S(2)}) collective-permute-start(bf16[4,128,256]{2,1,0:T(8,128)(2,1)S(1)} %pad_maximum_fusion.2.refs_0_), channel_id=1, source_target_pairs={{0,8},{1,3},{2,10},{3,5},{4,12},{5,7},{6,14},{7,1},{8,16},{9,11},{... | collective-permute-start | bytes 786440 | tf_op jit(solution)/shard_map/ppermute | solution.py:48
  90.7 12.4 %collective-permute-start.29 = (bf16[2,64,512]{2,1,0:T(8,128)(2,1)S(1)}, bf16[2,64,512]{2,1,0:T(8,128)(2,1)}, u32[]{:S(2)}, u32[]{:S(2)}) collective-permute-start(bf16[2,64,512]{2,1,0:T(8,128)(2,1)S(1)} %pad_maximum_fusion.5), channel_id=1, source_target_pairs={{0,32},{32,0},{64,96},{96,64},{1,33},{33,1},{65,97},{97,65},{2,34}... | collective-permute-start | bytes 393224 | tf_op jit(solution)/shard_map/ppermute | solution.py:56
  92.2 12.0 %collective-permute-start.25 = (bf16[256,256]{1,0:T(8,128)(2,1)S(1)}, bf16[256,256]{1,0:T(8,128)(2,1)S(1)}, u32[]{:S(2)}, u32[]{:S(2)}) collective-permute-start(bf16[256,256]{1,0:T(8,128)(2,1)S(1)} %copy-done.8), channel_id=1, source_target_pairs={{0,1},{1,0},{2,3},{3,2},{4,5},{5,4},{6,7},{7,6},{8,9},{9,8},{10,11... | collective-permute-start | bytes 393224 | tf_op jit(solution)/shard_map/ppermute | solution.py:52
  96.2 13.0 %collective-permute-start.30 = (bf16[4,128,256]{2,1,0:T(8,128)(2,1)S(1)}, bf16[4,128,256]{2,1,0:T(8,128)(2,1)S(1)}, u32[]{:S(2)}, u32[]{:S(2)}) collective-permute-start(bf16[4,128,256]{2,1,0:T(8,128)(2,1)S(1)} %pad_maximum_fusion.2.refs_0_), channel_id=1, source_target_pairs={{0,1},{1,0},{2,3},{3,2},{4,5},{5,4},{6,7},{7,6},{8,9},{9,8},{10,11... | collective-permute-start | bytes 786440 | tf_op jit(solution)/shard_map/ppermute | solution.py:52
  97.1 12.0 %collective-permute-start.33 = (bf16[4,128,256]{2,1,0:T(8,128)(2,1)S(1)}, bf16[4,128,256]{2,1,0:T(8,128)(2,1)S(1)}, u32[]{:S(2)}, u32[]{:S(2)}) collective-permute-start(bf16[4,128,256]{2,1,0:T(8,128)(2,1)S(1)} %collective-permute-done.24.refs_3_), channel_id=1, source_target_pairs={{0,1},{1,0},{2,3},{3,2},{4,5},{5,4},{6,7},{7,6},{8,9},{9,8},{10,11... | collective-permute-start | bytes 786440 | tf_op jit(solution)/shard_map/ppermute | solution.py:52
  100.4 8.8 %collective-permute-start.32 = (bf16[4,128,256]{2,1,0:T(8,128)(2,1)S(1)}, bf16[4,128,256]{2,1,0:T(8,128)(2,1)S(1)}, u32[]{:S(2)}, u32[]{:S(2)}) collective-permute-start(bf16[4,128,256]{2,1,0:T(8,128)(2,1)S(1)} %collective-permute-done.23.refs_2_), channel_id=1, source_target_pairs={{0,1},{1,0},{2,3},{3,2},{4,5},{5,4},{6,7},{7,6},{8,9},{9,8},{10,11... | collective-permute-start | bytes 786440 | tf_op jit(solution)/shard_map/ppermute | solution.py:52
  103.1 6.1 %collective-permute-start.31 = (bf16[4,128,256]{2,1,0:T(8,128)(2,1)S(1)}, bf16[4,128,256]{2,1,0:T(8,128)(2,1)S(1)}, u32[]{:S(2)}, u32[]{:S(2)}) collective-permute-start(bf16[4,128,256]{2,1,0:T(8,128)(2,1)S(1)} %collective-permute-done.22.refs_1_), channel_id=1, source_target_pairs={{0,1},{1,0},{2,3},{3,2},{4,5},{5,4},{6,7},{7,6},{8,9},{9,8},{10,11... | collective-permute-start | bytes 786440 | tf_op jit(solution)/shard_map/ppermute | solution.py:52
  (18 other events, 239.2 us)
